TPU v7x, 128 devices: a whole 4x4x4 slice. The times are simulated.
128 devices in a mesh: seq: 32 (over y, z, core), head: 4 (over x).
Axes of the slice: x: 4, y: 4, z: 4, core: 2. Of those that a mesh axis runs over, the one named last changes fastest.
Arguments:
- queries: bfloat16 [32768, 16, 128], P('seq', 'head'), may hold values from -8 to 8
- key_rows: bfloat16 [32768, 16, 128], P('seq', 'head'), may hold values from -8 to 8
- value_rows: bfloat16 [32768, 16, 128], P('seq', 'head'), may hold values from -6 to 6
- out_grad: bfloat16 [32768, 16, 128], P('seq', 'head'), may hold values from -6 to 6
- bucket_id: int32 [32768, 16], P('seq', 'head'), may hold values from 0 to 63, as said below
- bucket_slot: int32 [32768, 16], P('seq', 'head'), may hold values from 0 to 31, as said below
Outputs:
- attended: bfloat16 [32768, 16, 128], P('seq', 'head')
- grad_query: bfloat16 [32768, 16, 128], P('seq', 'head')
- grad_key: bfloat16 [32768, 16, 128], P('seq', 'head')
- grad_value: bfloat16 [32768, 16, 128], P('seq', 'head')
Inputs may be any that keep to these rules, and one draw needn't show every extreme that they name: `bucket_id`: for each head and each device's 1024 tokens, at most 32 tokens name one bucket; in every head one bucket is named by exactly 32 tokens of every device. `bucket_slot`: tokens of one device with the same head and bucket have distinct slots, increasing with the token index.
All inputs are finite; a program needn't handle non-finite values.
Results may differ from a plain program's by a relative error of at most 0.013.
The roundings to bfloat16 on the way count: a program that leaves them out, or rounds other values in their place, can miss the bound.
Values may be sent and summed in bfloat16 or wider, within the bound.
A program may use at most 128 MiB of HBM per device.

v0:
```python
import math

import jax
import jax.numpy as jnp
from jax import lax
from jax.sharding import PartitionSpec as P

SLOTS_PER_SOURCE = 32
BUCKETS_PER_HEAD = 64


def bucket_weights(q_part, k_part, valid, scale):
    span = q_part.shape[0]
    sorted_index = jnp.arange(span, dtype=jnp.int32)
    allowed = (sorted_index[None, :] <= sorted_index[:, None]) & (
        (valid[None, :] > 0) | (sorted_index[None, :] == sorted_index[:, None])
    )
    scores = jnp.dot(q_part, k_part.T, preferred_element_type=jnp.float32) * scale
    scores = jnp.where(allowed, scores, jnp.float32(-1e30))
    top = jnp.max(scores, axis=1, keepdims=True)
    expd = jnp.where(allowed, jnp.exp(scores - top), jnp.float32(0.0))
    return expd / jnp.sum(expd, axis=1, keepdims=True)


def bucket_forward(block, valid, width):
    scale = 1.0 / math.sqrt(width)
    weights = bucket_weights(block[:, :width], block[:, width : 2 * width], valid, scale)
    rounded = weights.astype(jnp.bfloat16)
    return jnp.dot(rounded, block[:, 2 * width :], preferred_element_type=jnp.float32).astype(
        jnp.bfloat16
    )


def bucket_backward(block, d_part, valid, width):
    scale = 1.0 / math.sqrt(width)
    q_part = block[:, :width]
    k_part = block[:, width : 2 * width]
    v_part = block[:, 2 * width : 3 * width]
    weights = bucket_weights(q_part, k_part, valid, scale)
    rounded = weights.astype(jnp.bfloat16)
    dprob = jnp.dot(d_part, v_part.T, preferred_element_type=jnp.float32)
    delta = jnp.sum(weights * dprob, axis=1, keepdims=True)
    dscore = (weights * (dprob - delta)).astype(jnp.bfloat16)
    grad_q = (jnp.dot(dscore, k_part, preferred_element_type=jnp.float32) * scale).astype(
        jnp.bfloat16
    )
    grad_k = (jnp.dot(dscore.T, q_part, preferred_element_type=jnp.float32) * scale).astype(
        jnp.bfloat16
    )
    grad_v = jnp.dot(rounded.T, d_part, preferred_element_type=jnp.float32).astype(jnp.bfloat16)
    return (rounded, v_part, grad_q, grad_k, grad_v)


def bucket_grads(block, d_part, valid, width):
    rounded, v_part, grad_q, grad_k, grad_v = bucket_backward(block, d_part, valid, width)
    return jnp.concatenate([grad_q, grad_k, grad_v], axis=1)


def shards(queries, key_rows, value_rows, out_grad, bucket_id, bucket_slot):
    peers = lax.axis_size("seq")
    tok_count, group, width = queries.shape
    per_owner = BUCKETS_PER_HEAD // peers
    span = peers * SLOTS_PER_SOURCE
    total = group * per_owner * span
    owner = bucket_id // per_owner
    local_bucket = bucket_id % per_owner
    head_index = jnp.arange(group, dtype=jnp.int32)[None, :]
    flat = (
        (head_index * per_owner + local_bucket) * span + owner * SLOTS_PER_SOURCE + bucket_slot
    ).reshape(-1)
    marks = (
        jnp.zeros((total,), jnp.bfloat16)
        .at[flat]
        .set(jnp.bfloat16(1.0))
        .reshape(group, per_owner, span)
    )

    def spread(rows):
        columns = rows.shape[-1]
        placed = jnp.zeros((total, columns), rows.dtype).at[flat].set(rows.reshape(-1, columns))
        return placed.reshape(group, per_owner, span, columns)

    def collect(buffer):
        columns = buffer.shape[-1]
        return buffer.reshape(total, columns)[flat].reshape(tok_count, group, columns)

    joined = jnp.concatenate([queries, key_rows, value_rows], axis=2)
    blocks, valid = (
        lax.all_to_all(spread(joined), "seq", split_axis=2, concat_axis=2, tiled=True),
        lax.all_to_all(marks, "seq", split_axis=2, concat_axis=2, tiled=True),
    )
    flat_blocks = blocks.reshape(-1, span, 3 * width)
    flat_valid = valid.reshape(-1, span)
    attended = lax.map(
        lambda item: bucket_forward(item[0], item[1], width), (flat_blocks, flat_valid)
    )
    attended = lax.all_to_all(
        attended.reshape(group, per_owner, span, width),
        "seq",
        split_axis=2,
        concat_axis=2,
        tiled=True,
    )
    incoming = lax.all_to_all(spread(out_grad), "seq", split_axis=2, concat_axis=2, tiled=True)
    grads = lax.map(
        lambda item: bucket_grads(item[0], item[1], item[2], width),
        (flat_blocks, incoming.reshape(-1, span, width), flat_valid),
    )
    grads = lax.all_to_all(
        grads.reshape(group, per_owner, span, 3 * width),
        "seq",
        split_axis=2,
        concat_axis=2,
        tiled=True,
    )
    gathered = collect(grads)
    return (
        collect(attended),
        gathered[:, :, :width],
        gathered[:, :, width : 2 * width],
        gathered[:, :, 2 * width :],
    )


def solution(mesh):
    in_specs = (
        P("seq", "head", None),
        P("seq", "head", None),
        P("seq", "head", None),
        P("seq", "head", None),
        P("seq", "head"),
        P("seq", "head"),
    )
    out_specs = (
        P("seq", "head", None),
        P("seq", "head", None),
        P("seq", "head", None),
        P("seq", "head", None),
    )
    return jax.shard_map(shards, mesh=mesh, in_specs=in_specs, out_specs=out_specs, check_vma=False)
```

profile of v0, /device:TPU:32, one launch (start us, length us, event | category | flops | bytes accessed | tf_op | source)
XLA Modules:
  0.0 543.0 jit_solution(14377481210487384472)
XLA Ops:
  2.1 28.6 %scatter_custom_fusion = bf16[8192]{0:T(1024)(128)(2,1)S(1)} fusion(s32[4096]{0:T(1024)S(1)} %bitcast.59, bf16[4096]{0:T(1024)(128)(2,1)S(1)} %broadcast.63, bf16[]{:T(256)} %constant.78.clone.1), kind=kCustom, calls=%fused_computation.82 | custom fusion | bytes 16386 | tf_op jit(solution)/shard_map/scatter | solution.py:74
  32.6 8.2 %all-to-all-start = ((bf16[32,2,128]{2,1,0:T(2,128)(2,1)}), bf16[32,2,128]{2,1,0:T(2,128)(2,1)S(1)}, u32[]{:S(2)}, u32[]{:S(2)}) async-start(bf16[32,2,128]{2,1,0:T(2,128)(2,1)} %reshape.154), calls=%async_computation | async-start | bytes 32768 | tf_op jit(solution)/shard_map/all_to_all | solution.py:90
  40.8 11.9 %scatter_custom_fusion.2 = bf16[8192,128]{1,0:T(8,128)(2,1)S(1)} fusion(s32[4096]{0:T(1024)S(1)} %bitcast.60, bf16[4096,128]{1,0:T(8,128)(2,1)} %bitcast.63, bf16[]{:T(256)} %constant.78.clone.1), kind=kCustom, calls=%fused_computation.65 | custom fusion | bytes 2097664 | tf_op jit(solution)/shard_map/scatter | solution.py:80
  56.2 7.9 %all-to-all-start.3 = ((bf16[4,2,1024,128]{3,1,0,2:T(2,128)(2,1)}), bf16[4,2,1024,128]{3,1,0,2:T(2,128)(2,1)}, u32[]{:S(2)}, u32[]{:S(2)}) async-start(bf16[4,2,1024,128]{3,1,0,2:T(2,128)(2,1)} %copy.42), calls=%async_computation.3 | async-start | bytes 4194304 | tf_op jit(solution)/shard_map/all_to_all | solution.py:104
  70.2 22.2 %scatter_custom_fusion.1 = bf16[8192,384]{1,0:T(8,128)(2,1)} fusion(s32[4096]{0:T(1024)S(1)} %bitcast.61, bf16[4096,384]{1,0:T(8,128)(2,1)} %reshape.134, bf16[]{:T(256)} %constant.78.clone.1), kind=kCustom, calls=%fused_computation.63 | custom fusion | bytes 6291968 | tf_op jit(solution)/shard_map/scatter | solution.py:80
  92.4 12.7 %copy.38 = bf16[4,2,1024,384]{3,1,0,2:T(2,128)(2,1)} copy(bf16[4,2,1024,384]{3,2,1,0:T(8,128)(2,1)} %bitcast.53) | data formatting | bytes 12582912 | tf_op jit(solution)/shard_map/reshape | solution.py:81
  105.2 8.1 %all-to-all-start.1 = ((bf16[4,2,1024,384]{3,1,0,2:T(2,128)(2,1)}), bf16[4,2,1024,384]{3,1,0,2:T(2,128)(2,1)}, u32[]{:S(2)}, u32[]{:S(2)}) async-start(bf16[4,2,1024,384]{3,1,0,2:T(2,128)(2,1)} %copy.38), calls=%async_computation.1 | async-start | bytes 12582912 | tf_op jit(solution)/shard_map/all_to_all | solution.py:89
  118.1 82.2 %all-to-all-done.1 = bf16[4,2,1024,384]{3,1,0,2:T(2,128)(2,1)} async-done(((bf16[4,2,1024,384]{3,1,0,2:T(2,128)(2,1)}), bf16[4,2,1024,384]{3,1,0,2:T(2,128)(2,1)}, u32[]{:S(2)}, u32[]{:S(2)}) %all-to-all-start.1) | async-done | bytes 6291488 | tf_op jit(solution)/shard_map/all_to_all | solution.py:89
  200.3 6.3 %copy.48 = bf16[4,2,1024,384]{3,2,1,0:T(8,128)(2,1)} copy(bf16[4,2,1024,384]{3,1,0,2:T(2,128)(2,1)} %all-to-all-done.1) | data formatting | bytes 12582912 | tf_op jit(solution)/shard_map/while | solution.py:94
  206.5 50.2 %while.20 = (s32[]{:T(128)}, bf16[8,1024,128]{2,1,0:T(8,128)(2,1)S(1)}, bf16[8,1024]{1,0:T(8,128)(2,1)S(1)}, bf16[8,1024,384]{2,1,0:T(8,128)(2,1)}, s32[]{:T(128)}) while((s32[]{:T(128)}, bf16[8,1024,128]{2,1,0:T(8,128)(2,1)S(1)}, bf16[8,1024]{1,0:T(8,128)(2,1)S(1)}, bf16[8,1024,384]{2,1,0:T(8,128)(2,1)}, s32[]{:T(128)}) %tuple.58), condition=%wide.region_5.6_spmd, body=%wide.region_2.5_spmd.sunk | while | flops 564265984 | bytes 15231049 | solution.py:94
  259.5 5.4 all-to-all-start.2
  264.9 134.7 %while.21 = (s32[]{:T(128)}, bf16[8,1024,384]{1,2,0:T(8,128)(2,1)}, bf16[8,1024]{1,0:T(8,128)(2,1)S(1)}, bf16[8,1024,384]{2,1,0:T(8,128)(2,1)}, bf16[8,1024,128]{2,1,0:T(8,128)(2,1)}, /*index=5*/s32[]{:T(128)}) while((s32[]{:T(128)}, bf16[8,1024,384]{1,2,0:T(8,128)(2,1)}, bf16[8,1024]{1,0:T(8,128)(2,1)S(1)}, ...), condition=%wide.region_11.12_spmd, body=%wide.region_7.11_spmd.sunk | while | flops 1396572160 | bytes 41473612 | solution.py:105
  276.6 4.2 fusion.86
  293.4 4.2 fusion.86
  310.2 4.2 fusion.86
  327.1 4.2 fusion.86
  344.0 4.2 fusion.86
  399.6 16.4 %copy.47 = bf16[4,2,1024,384]{3,1,0,2:T(2,128)(2,1)} copy(bf16[4,2,1024,384]{2,3,1,0:T(8,128)(2,1)} %bitcast.13) | data formatting | bytes 12582912 | tf_op jit(solution)/shard_map/reshape | solution.py:110
  417.4 7.8 %all-to-all-start.4 = ((bf16[4,2,1024,384]{3,1,0,2:T(2,128)(2,1)}), bf16[4,2,1024,384]{3,1,0,2:T(2,128)(2,1)}, u32[]{:S(2)}, u32[]{:S(2)}) async-start(bf16[4,2,1024,384]{3,1,0,2:T(2,128)(2,1)} %copy.47), calls=%async_computation.4 | async-start | bytes 12582912 | tf_op jit(solution)/shard_map/all_to_all | solution.py:109
  427.1 15.0 %gather_fusion = bf16[4096,128]{1,0:T(8,128)(2,1)} fusion(bf16[8192,128]{1,0:T(8,128)(2,1)S(1)} %bitcast.51, s32[4096]{0:T(1024)S(1)} %broadcast_clamp_fusion), kind=kCustom, calls=%fused_computation | custom fusion | bytes 2113536 | tf_op jit(solution)/shard_map/gather | solution.py:85
  442.1 70.0 %all-to-all-done.4 = bf16[4,2,1024,384]{3,1,0,2:T(2,128)(2,1)} async-done(((bf16[4,2,1024,384]{3,1,0,2:T(2,128)(2,1)}), bf16[4,2,1024,384]{3,1,0,2:T(2,128)(2,1)}, u32[]{:S(2)}, u32[]{:S(2)}) %all-to-all-start.4) | async-done | bytes 6291488 | tf_op jit(solution)/shard_map/all_to_all | solution.py:109
  512.1 6.3 %copy.46 = bf16[4,2,1024,384]{3,2,1,0:T(8,128)(2,1)} copy(bf16[4,2,1024,384]{3,1,0,2:T(2,128)(2,1)} %all-to-all-done.4) | data formatting | bytes 12582912 | tf_op jit(solution)/shard_map/all_to_all | solution.py:109
  518.4 17.6 %gather_fusion.1 = bf16[4096,384]{1,0:T(8,128)(2,1)S(1)} fusion(bf16[8192,384]{1,0:T(8,128)(2,1)} %bitcast.50, s32[4096]{0:T(1024)S(1)} %broadcast_clamp_fusion), kind=kCustom, calls=%fused_computation.1 | custom fusion | bytes 6307840 | tf_op jit(solution)/shard_map/gather | solution.py:85
  538.5 4.2 fusion.55
  (146 shorter events, 189.3 us)
Async XLA Ops:
  2.1 68.2 %copy-start.1 = (s32[4096,1]{0,1:T(1,128)}, s32[4096,1]{0,1:T(1,128)S(1)}, u32[]{:S(2)}) copy-start(s32[4096,1]{0,1:T(1,128)S(1)} %compare_select_fusion) | copy-start | bytes 49156
  32.6 23.6 %all-to-all-start = ((bf16[32,2,128]{2,1,0:T(2,128)(2,1)}), bf16[32,2,128]{2,1,0:T(2,128)(2,1)S(1)}, u32[]{:S(2)}, u32[]{:S(2)}) async-start(bf16[32,2,128]{2,1,0:T(2,128)(2,1)} %reshape.154), calls=%async_computation | async-start | bytes 32768 | tf_op jit(solution)/shard_map/all_to_all | solution.py:90
  56.2 49.0 %all-to-all-start.3 = ((bf16[4,2,1024,128]{3,1,0,2:T(2,128)(2,1)}), bf16[4,2,1024,128]{3,1,0,2:T(2,128)(2,1)}, u32[]{:S(2)}, u32[]{:S(2)}) async-start(bf16[4,2,1024,128]{3,1,0,2:T(2,128)(2,1)} %copy.42), calls=%async_computation.3 | async-start | bytes 4194304 | tf_op jit(solution)/shard_map/all_to_all | solution.py:104
  105.2 95.1 %all-to-all-start.1 = ((bf16[4,2,1024,384]{3,1,0,2:T(2,128)(2,1)}), bf16[4,2,1024,384]{3,1,0,2:T(2,128)(2,1)}, u32[]{:S(2)}, u32[]{:S(2)}) async-start(bf16[4,2,1024,384]{3,1,0,2:T(2,128)(2,1)} %copy.38), calls=%async_computation.1 | async-start | bytes 12582912 | tf_op jit(solution)/shard_map/all_to_all | solution.py:89
  259.5 156.5 %all-to-all-start.2 = ((bf16[4,2,1024,128]{3,1,0,2:T(2,128)(2,1)}), bf16[4,2,1024,128]{3,1,0,2:T(2,128)(2,1)S(1)}, u32[]{:S(2)}, u32[]{:S(2)}) async-start(bf16[4,2,1024,128]{3,1,0,2:T(2,128)(2,1)} %bitcast.54), calls=%async_computation.2 | async-start | bytes 4194304 | tf_op jit(solution)/shard_map/all_to_all | solution.py:97
  416.0 9.2 %copy-start.2 = (s32[4096,1]{0,1:T(1,128)S(1)}, s32[4096,1]{0,1:T(1,128)}, u32[]{:S(2)}) copy-start(s32[4096,1]{0,1:T(1,128)} %copy-done.1) | copy-start | bytes 49156
  416.0 1.4 copy-start
  417.4 94.7 %all-to-all-start.4 = ((bf16[4,2,1024,384]{3,1,0,2:T(2,128)(2,1)}), bf16[4,2,1024,384]{3,1,0,2:T(2,128)(2,1)}, u32[]{:S(2)}, u32[]{:S(2)}) async-start(bf16[4,2,1024,384]{3,1,0,2:T(2,128)(2,1)} %copy.47), calls=%async_computation.4 | async-start | bytes 12582912 | tf_op jit(solution)/shard_map/all_to_all | solution.py:109
where the time goes:
time: 553 us; the launch traced here: 543 us
  local copies, waits for them, and re-layouts  182 us (33%)
  waiting for transfers between devices  152 us (27%)
  matrix products  85.3 us (15%)
  other arithmetic  84.1 us (15%)
  starting transfers between devices  37.4 us (7%)
    all_to_all x1, waiting for transfers between devices, shards(): lax.all_to_all(spread(joined), 'seq', split_axis=2, concat_axis=2, tiled=...  82.2 us
    all_to_all x1, waiting for transfers between devices, shards(): lax.all_to_all(grads.reshape(group, per_owner, span, 3 * width), 'seq', s...  70 us
    reduce_sum x16, other arithmetic, bucket_weights(): return expd / jnp.sum(expd, axis=1, keepdims=True)  45.1 us
    scatter x2, local copies, waits for them, and re-layouts, spread(): jnp.zeros((total, columns), rows.dtype).at[flat]  34.1 us
    dot_general x8, matrix products, bucket_backward(): jnp.dot(rounded.T, d_part, preferred_element_type=jnp.float32)  33.5 us
    gather x2, local copies, waits for them, and re-layouts, collect(): buffer.reshape(total, columns)[flat].reshape(tok_count, group, columns)  32.7 us
    scatter x1, local copies, waits for them, and re-layouts, shards(): marks = jnp.zeros((total,), jnp.bfloat16).at[flat].set(jnp.bfloat16(1.0))...  28.6 us
    convert_element_type x8, other arithmetic, bucket_backward(): dscore = (weights * (dprob - delta)).astype(jnp.bfloat16)  26.3 us
  transfers between devices with their start and end apart: 5, of which 2 were waited for; matrix products, arithmetic and copies ran while one was open for 42% of the time, Pallas kernels for 0%

commit v1 on v0

--- a/solution.py
+++ b/solution.py
@@ -1,33 +1,593 @@
+import functools
 import math
 
 import jax
 import jax.numpy as jnp
 from jax import lax
+from jax.experimental import pallas as pl
+from jax.experimental.pallas import tpu as pltpu
 from jax.sharding import PartitionSpec as P
 
 SLOTS_PER_SOURCE = 32
 BUCKETS_PER_HEAD = 64
+PEERS = 32
+ROWS = 96
+SPAN = PEERS * ROWS
+HOT_ROWS = PEERS * SLOTS_PER_SOURCE
+HOT_AT = (0, 10, 20, 30)
+TQ, TK = 256, 512
+FAR = 2.0**100
+MESH = pl.DeviceIdType.MESH
+F32, BF16, I32 = jnp.float32, jnp.bfloat16, jnp.int32
+
+
+def both(chips):
+    return [(dy, dz, dc) for dy, dz in chips for dc in (0, 1)]
+
+
+FAR_MIX = [(1, 2), (3, 2), (2, 1), (2, 3)]
+NEAR = [(1, 0), (3, 0), (0, 1), (0, 3)]
+ROUNDS = [
+    [(dy, dz, 0) for dy, dz in FAR_MIX],
+    [(dy, dz, 1) for dy, dz in FAR_MIX],
+    both([(2, 2)]),
+    both([(1, 3), (3, 1)]),
+    both([(1, 1), (3, 3)]),
+    both([(2, 0), (0, 2)]),
+    [(dy, dz, 0) for dy, dz in NEAR],
+    [(dy, dz, 1) for dy, dz in NEAR] + [(0, 0, 1)],
+]
+OFFSETS = [o for r in ROUNDS for o in r]
+FIRST = [sum(len(r) for r in ROUNDS[:i]) for i in range(len(ROUNDS))]
+LAG = 2
+
+
+def iota(shape, dim):
+    return lax.broadcasted_iota(I32, shape, dim)
+
+
+def dot(a, b, dims=((1,), (0,))):
+    return lax.dot_general(a, b, (dims, ((), ())), preferred_element_type=F32)
+
+
+def kernel(
+    q_ref, k_ref, v_ref, d_ref, bid_ref,
+    o_q, o_k, o_v, o_d, flag_out,
+    wide, x, send, send_hot, recv, recv_hot, ret, ret_hot, meta, meta_in, flags,
+    pos_row, pos_col, aug_q, aug_k, kt, vt, dk, dv, s_buf, p_buf, acc_o, acc_q,
+    send_sem, recv_sem, meta_ssem, meta_rsem, hot_ssem, hot_rsem, back_ssem, back_rsem,
+    flag_ssem, flag_rsem, own_sem,
+):
+    me = lax.axis_index("seq")
+    col = lax.axis_index("head")
+    y, z, c = me // 8, lax.rem(me // 2, 4), lax.rem(me, 2)
+    scale = 1.0 / math.sqrt(128)
+    to_exp2 = scale * math.log2(math.e)
+
+    def peer(o, sign=1):
+        return (
+            lax.rem(y + sign * o[0] + 4, 4) * 8
+            + lax.rem(z + sign * o[1] + 4, 4) * 2
+            + lax.rem(c + o[2], 2)
+        )
+
+    barrier = pltpu.get_barrier_semaphore()
+    for o in OFFSETS:
+        pl.semaphore_signal(barrier, inc=1, device_id={"seq": peer(o)}, device_id_type=MESH)
+    for step in (1, 2, 3):
+        pl.semaphore_signal(
+            barrier, inc=1, device_id={"head": lax.rem(col + step, 4)}, device_id_type=MESH
+        )
+
+    for a, ref in enumerate((q_ref, k_ref, v_ref, d_ref)):
+        wide[...] = ref[...].astype(F32)
+        for h in range(4):
+            x[h // 2, pl.ds(h % 2 * 1024, 1024), a * 128 : a * 128 + 128] = wide[
+                pl.ds(h, 1024, stride=4), :
+            ].astype(BF16)
+
+    def row_facts(shape):
+        r = iota(shape, 0)
+        return r // 64, lax.rem(r, 64)
+
+    named = jnp.concatenate(
+        [(iota((64, 1024), 0) == bid_ref[h : h + 1, :]).astype(F32) for h in range(4)], axis=0
+    )
+    earlier = (iota((1024, 1024), 0) < iota((1024, 1024), 1)).astype(F32).astype(BF16)
+    rank = dot(named.astype(BF16), earlier)
+    count = jnp.sum(named, axis=1, keepdims=True)
+    full = (count == 32.0).astype(F32)
+    count = count * (1.0 - full)
+    bad = jnp.float32(0.0)
+    for h in range(4):
+        n_full = jnp.sum(full[h * 64 : h * 64 + 64])
+        bad = jnp.maximum(bad, (n_full != 1.0).astype(F32))
+    r0, r1 = iota((256, 256), 0), iota((256, 256), 1)
+
+    def code_of(r):
+        return lax.rem(r // 64, 2) * 2 + lax.rem(r, 2)
+
+    def place_of(r):
+        return (r // 128) * 32 + lax.rem(r, 64) // 2
+
+    before = ((place_of(r0) == place_of(r1)) & (code_of(r1) < code_of(r0))).astype(F32).astype(BF16)
+    lanes = jnp.broadcast_to(count, (256, 128))
+    start = dot(before, lanes.astype(BF16))[:, :1]
+    rows = iota((256, 1), 0)
+    base = (lax.rem(rows, 64) // 2 * ROWS).astype(F32) + start
+    hot_base = (SPAN + lax.rem(rows // 64, 2) * 32).astype(F32)
+    base = jnp.where(full > 0, hot_base, base)
+    landed = named * (rank + base)
+    place = jnp.concatenate(
+        [jnp.sum(landed[h * 64 : h * 64 + 64], axis=0, keepdims=True) for h in range(4)]
+        + [jnp.zeros((124, 1024), F32)],
+        axis=0,
+    )
+    pos_row[...] = place[:8].astype(I32)
+    pos_col[...] = place.T.astype(I32)
+
+    lane = iota((256, 128), 1)
+    code = code_of(iota((256, 128), 0))
+    w_start = jnp.where((lane <= 4) & (code < lane), lanes, 0.0).astype(BF16)
+    w_end = jnp.where((lane < 4) & (code <= lane), lanes, 0.0).astype(BF16)
+    mr, mc = iota((512, 256), 0), iota((512, 256), 1)
+    mine = mr // 16 == lax.rem(mc, 64) // 2
+    pick_start = (mine & (lax.rem(mr, 16) == mc // 128 * 2)).astype(F32).astype(BF16)
+    pick_end = (mine & (lax.rem(mr, 16) == mc // 128 * 2 + 1)).astype(F32).astype(BF16)
+    starts = dot(pick_start, w_start)
+    bad = jnp.maximum(bad, (jnp.max(starts) > ROWS).astype(F32))
+    kind, ml = lax.rem(iota((512, 128), 0), 16), iota((512, 128), 1)
+    tail = jnp.where(((kind == 1) | (kind == 3)) & (ml == 4), jnp.float32(ROWS), 0.0)
+    tail = tail + jnp.where(kind == 4, bad, 0.0)
+    meta[...] = (starts + dot(pick_end, w_end) + tail).astype(BF16)
+
+    pl.semaphore_wait(barrier, len(OFFSETS) + 3)
+
+    def meta_copy(k):
+        return pltpu.make_async_remote_copy(
+            src_ref=meta.at[pl.ds(pl.multiple_of(peer(OFFSETS[k]) * 16, 16), 16)],
+            dst_ref=meta_in.at[pl.ds(pl.multiple_of(me * 16, 16), 16)],
+            send_sem=meta_ssem.at[k],
+            recv_sem=meta_rsem.at[k],
+            device_id={"seq": peer(OFFSETS[k])},
+            device_id_type=MESH,
+        )
+
+    for k in range(len(OFFSETS)):
+        meta_copy(k).start()
+    own_meta = pl.ds(pl.multiple_of(me * 16, 16), 16)
+    meta_in[own_meta, :] = meta[own_meta, :]
+
+    own = pl.ds(pl.multiple_of(me * ROWS, ROWS), ROWS)
+
+    def copy(phase, k):
+        other = peer(OFFSETS[k])
+        theirs = pl.ds(pl.multiple_of(other * ROWS, ROWS), ROWS)
+        g = phase % 2
+        src, dst = (send, recv) if phase < 2 else (recv, ret)
+        return pltpu.make_async_remote_copy(
+            src_ref=src.at[g, theirs],
+            dst_ref=dst.at[g, own],
+            send_sem=send_sem.at[phase, k],
+            recv_sem=recv_sem.at[phase, k],
+            device_id={"seq": other},
+            device_id_type=MESH,
+        )
+
+    def own_copy(phase):
+        g = phase % 2
+        src, dst = (send, recv) if phase < 2 else (recv, ret)
+        return pltpu.make_async_copy(src.at[g, own], dst.at[g, own], own_sem.at[phase])
+
+    def hot_copy(h):
+        return pltpu.make_async_remote_copy(
+            src_ref=send_hot.at[h // 2, pl.ds(h % 2 * 32, 32)],
+            dst_ref=recv_hot.at[pl.ds(pl.multiple_of(me * 32, 32), 32)],
+            send_sem=hot_ssem.at[h],
+            recv_sem=hot_rsem.at[me],
+            device_id={"seq": HOT_AT[h]},
+            device_id_type=MESH,
+        )
+
+    def hot_from(h, s):
+        return pltpu.make_async_remote_copy(
+            src_ref=send_hot.at[h // 2, pl.ds(h % 2 * 32, 32)],
+            dst_ref=recv_hot.at[pl.ds(s * 32, 32)],
+            send_sem=hot_ssem.at[h],
+            recv_sem=hot_rsem.at[s],
+            device_id={"seq": HOT_AT[h]},
+            device_id_type=MESH,
+        )
+
+    def hot_own(h):
+        return pltpu.make_async_copy(
+            send_hot.at[h // 2, pl.ds(h % 2 * 32, 32)],
+            recv_hot.at[pl.ds(HOT_AT[h] * 32, 32)],
+            hot_ssem.at[h],
+        )
+
+    def back_copy(h, s):
+        return pltpu.make_async_remote_copy(
+            src_ref=recv_hot.at[pl.ds(s * 32, 32)],
+            dst_ref=ret_hot.at[h // 2, pl.ds(h % 2 * 32, 32)],
+            send_sem=back_ssem.at[s],
+            recv_sem=back_rsem.at[h],
+            device_id={"seq": s},
+            device_id_type=MESH,
+        )
+
+    def back_own(h):
+        return pltpu.make_async_copy(
+            recv_hot.at[pl.ds(HOT_AT[h] * 32, 32)],
+            ret_hot.at[h // 2, pl.ds(h % 2 * 32, 32)],
+            back_rsem.at[h],
+        )
+
+    def issue(phase, r):
+        if r >= LAG:
+            for k in range(FIRST[r - LAG], FIRST[r - LAG] + len(ROUNDS[r - LAG])):
+                copy(phase, k).wait_send()
+        if r == 0:
+            own_copy(phase).start()
+        for k in range(FIRST[r], FIRST[r] + len(ROUNDS[r])):
+            copy(phase, k).start()
+        if r == len(ROUNDS) - 1:
+            g = phase % 2
+            for h in (2 * g, 2 * g + 1):
+                if phase < 2:
+
+                    @pl.when(me != HOT_AT[h])
+                    def _():
+                        hot_copy(h).start()
+
+                    @pl.when(me == HOT_AT[h])
+                    def _():
+                        hot_own(h).start()
+
+                else:
+
+                    @pl.when(me == HOT_AT[h])
+                    def _():
+                        for s in range(PEERS):
+                            if s != HOT_AT[h]:
+                                back_copy(h, s).start()
+                        back_own(h).start()
+
+    def drain_sends(phase):
+        for r in range(len(ROUNDS) - LAG, len(ROUNDS)):
+            for k in range(FIRST[r], FIRST[r] + len(ROUNDS[r])):
+                copy(phase, k).wait_send()
+        g = phase % 2
+        for h in (2 * g, 2 * g + 1):
+            if phase < 2:
+
+                @pl.when(me != HOT_AT[h])
+                def _():
+                    hot_copy(h).wait_send()
+
+            else:
+
+                @pl.when(me == HOT_AT[h])
+                def _():
+                    for s in range(PEERS):
+                        if s != HOT_AT[h]:
+                            back_copy(h, s).wait_send()
+
+    def arrive(phase):
+        for k in range(len(OFFSETS)):
+            copy(phase, k).wait_recv()
+        own_copy(phase).wait()
+
+    def hot_arrive(h):
+        for s in range(PEERS):
+            if s != HOT_AT[h]:
+                hot_from(h, s).wait_recv()
+        hot_own(h).wait()
+
+    def back_arrive(g):
+        for h in (2 * g, 2 * g + 1):
+
+            @pl.when(me != HOT_AT[h])
+            def _():
+                back_copy(h, 0).wait_recv()
+
+            @pl.when(me == HOT_AT[h])
+            def _():
+                back_own(h).wait()
+
+    def pack_hot(g):
+        at = jnp.concatenate([pos_row[2 * g : 2 * g + 1, :], pos_row[2 * g + 1 : 2 * g + 2, :]], axis=1)
+        pick = (iota((64, 2048), 0) + SPAN == at).astype(F32).astype(BF16)
+        send_hot[g] = dot(pick, x[g]).astype(BF16)
+
+    def pack(g, m):
+        at = jnp.concatenate([pos_row[2 * g : 2 * g + 1, :], pos_row[2 * g + 1 : 2 * g + 2, :]], axis=1)
+        pick = (iota((384, 2048), 0) == at - m * 384).astype(F32).astype(BF16)
+        send[g, pl.ds(pl.multiple_of(m * 384, 384), 384), :] = dot(pick, x[g]).astype(BF16)
+
+    def unpack(g, m):
+        h = m // 4
+        t = pl.ds(pl.multiple_of(lax.rem(m, 4) * 256, 256), 256)
+        at = jnp.where(h == 0, pos_col[t, 2 * g : 2 * g + 1], pos_col[t, 2 * g + 1 : 2 * g + 2])
+        pick = (iota((256, SPAN), 1) == at).astype(F32).astype(BF16)
+        hot_pick = (iota((256, 64), 1) + SPAN == at).astype(F32).astype(BF16)
+        got = dot(pick, ret[g]) + dot(hot_pick, ret_hot[g])
+        x[g, pl.ds(pl.multiple_of(m * 256, 256), 256), :] = got.astype(BF16)
+
+    def attend(rows_ref, span, coded, between):
+        def body(i, _):
+            between(i)
+            qs = pl.ds(pl.multiple_of(i * TQ, TQ), TQ)
+            q_i = rows_ref[qs, 0:128]
+            d_i = rows_ref[qs, 384:512]
+            q_a = jnp.concatenate([q_i, aug_q[qs, :]], axis=1) if coded else q_i
+            tiles = (i * TQ) // TK + 1
+
+            def score(j, top):
+                ks = pl.ds(pl.multiple_of(j * TK, TK), TK)
+                k_j = rows_ref[ks, 128:256]
+                if coded:
+                    k_j = jnp.concatenate([k_j, aug_k[ks, :]], axis=1)
+                s = dot(k_j, q_a, ((1,), (1,)))
+                gap = iota((TK, TQ), 0) - iota((TK, TQ), 1)
+                s = jnp.where(gap <= i * TQ - j * TK, s, -1e30)
+                s_buf[ks, :] = s
+                return jnp.maximum(top, jnp.max(s, axis=0, keepdims=True))
+
+            top = lax.fori_loop(0, tiles, score, jnp.full((1, TQ), -1e30, F32))
+
+            def weigh(j, sums):
+                total, delta = sums
+                ks = pl.ds(pl.multiple_of(j * TK, TK), TK)
+                p = jnp.exp2((s_buf[ks, :] - top) * to_exp2)
+                dp = dot(rows_ref[ks, 256:384], d_i, ((1,), (1,)))
+                s_buf[ks, :] = p
+                p_buf[ks, :] = dp
+                return (
+                    total + jnp.sum(p, axis=0, keepdims=True),
+                    delta + jnp.sum(p * dp, axis=0, keepdims=True),
+                )
+
+            none = jnp.zeros((1, TQ), F32)
+            total, delta = lax.fori_loop(0, tiles, weigh, (none, none))
+            inv = 1.0 / total
+            delta = delta * inv
+            acc_o[...] = jnp.zeros_like(acc_o)
+            acc_q[...] = jnp.zeros_like(acc_q)
+
+            def spread(j, _):
+                ks = pl.ds(pl.multiple_of(j * TK, TK), TK)
+                w = s_buf[ks, :] * inv
+                rounded = w.astype(BF16)
+                ds = (w * (p_buf[ks, :] - delta)).astype(BF16)
+                acc_o[...] += dot(vt[:, ks], rounded)
+                acc_q[...] += dot(kt[:, ks], ds)
+                dv[ks, :] += dot(rounded, d_i)
+                dk[ks, :] += dot(ds, q_i)
+                return 0
+
+            lax.fori_loop(0, tiles, spread, 0)
+            rows_ref[qs, 0:128] = acc_o[...].T.astype(BF16)
+            rows_ref[qs, 384:512] = (acc_q[...] * scale).T.astype(BF16)
+            return 0
+
+        def ready(j, _):
+            ks = pl.ds(pl.multiple_of(j * TK, TK), TK)
+            kt[:, ks] = rows_ref[ks, 128:256].astype(F32).T.astype(BF16)
+            vt[:, ks] = rows_ref[ks, 256:384].astype(F32).T.astype(BF16)
+            dk[ks, :] = jnp.zeros((TK, 128), F32)
+            dv[ks, :] = jnp.zeros((TK, 128), F32)
+            return 0
+
+        lax.fori_loop(0, span // TK, ready, 0)
+        lax.fori_loop(0, span // TQ, body, 0)
+
+        def finish(j, _):
+            ks = pl.ds(pl.multiple_of(j * TK, TK), TK)
+            rows_ref[ks, 128:256] = (dk[ks, :] * scale).astype(BF16)
+            rows_ref[ks, 256:384] = dv[ks, :].astype(BF16)
+            return 0
+
+        lax.fori_loop(0, span // TK, finish, 0)
+
+    def codes(g):
+        def body(s, _):
+            note = meta_in[pl.ds(pl.multiple_of(s * 16, 16), 16), :].astype(F32)
+            r = iota((ROWS, 128), 0).astype(F32)
+            inside = (r >= note[2 * g : 2 * g + 1]) & (r < note[2 * g + 1 : 2 * g + 2])
+            known = iota((ROWS, 128), 1) <= 4
+            at = pl.ds(pl.multiple_of(s * ROWS, ROWS), ROWS)
+            aug_q[at, :] = jnp.where(inside, 1.0, 0.0).astype(BF16)
+            aug_k[at, :] = jnp.where(known & ~inside, -FAR, 0.0).astype(BF16)
+            return 0
+
+        lax.fori_loop(0, PEERS, body, 0)
+
+    n_rounds = len(ROUNDS)
+
+    def hot_work(g):
+        for h in (2 * g, 2 * g + 1):
+
+            @pl.when(me == HOT_AT[h])
+            def _():
+                hot_arrive(h)
+                attend(recv_hot, HOT_ROWS, False, lambda i: None)
+
+    def pack_body(g):
+        def body(m, _):
+            pack(g, m)
+            return 0
+
+        lax.fori_loop(0, 8, body, 0)
+        pack_hot(g)
+
+    pack_body(0)
+    issue(0, 0)
+    issue(0, 1)
+
+    def pack_send(m, _):
+        pack(1, m)
+        for r in range(2, n_rounds):
+
+            @pl.when(m == r)
+            def _():
+                issue(0, r)
+
+        return 0
+
+    lax.fori_loop(0, 8, pack_send, 0)
+    pack_hot(1)
+
+    for k in range(len(OFFSETS)):
+        meta_copy(k).wait()
+    noted = meta_in[...].astype(F32)
+    noted = jnp.where(lax.rem(iota((512, 128), 0), 16) == 4, noted, 0.0)
+    flags[0] = jnp.broadcast_to(jnp.max(noted, axis=0, keepdims=True), (16, 128)).astype(BF16)
+
+    def flag_copy(step):
+        return pltpu.make_async_remote_copy(
+            src_ref=flags.at[0],
+            dst_ref=flags.at[step],
+            send_sem=flag_ssem.at[step],
+            recv_sem=flag_rsem.at[step],
+            device_id={"head": lax.rem(col + step, 4)},
+            device_id_type=MESH,
+        )
+
+    for step in (1, 2, 3):
+        flag_copy(step).start()
+
+    codes(0)
+    issue(1, 0)
+    issue(1, 1)
+    arrive(0)
+    drain_sends(0)
+
+    def between_to(phase):
+        def between(i):
+            for r in range(2, n_rounds):
+
+                @pl.when(i == r + 1)
+                def _():
+                    issue(phase, r)
+
+        return between
+
+    attend(recv.at[0], SPAN, True, between_to(1))
+    hot_work(0)
+    codes(1)
+    issue(2, 0)
+    issue(2, 1)
+    arrive(1)
+    drain_sends(1)
+    attend(recv.at[1], SPAN, True, between_to(2))
+    hot_work(1)
+    issue(3, 0)
+    issue(3, 1)
+    arrive(2)
+    back_arrive(0)
+    drain_sends(2)
+
+    def unpack_send(m, _):
+        unpack(0, m)
+        for r in range(2, n_rounds):
+
+            @pl.when(m == r)
+            def _():
+                issue(3, r)
+
+        return 0
+
+    lax.fori_loop(0, 8, unpack_send, 0)
+    for step in (1, 2, 3):
+        flag_copy(step).wait()
+    any_flag = jnp.maximum(
+        jnp.maximum(flags[0].astype(F32), flags[1].astype(F32)),
+        jnp.maximum(flags[2].astype(F32), flags[3].astype(F32)),
+    )
+    flag_out[...] = any_flag[:8]
+    arrive(3)
+    back_arrive(1)
+    drain_sends(3)
+
+    def unpack_last(m, _):
+        unpack(1, m)
+        return 0
+
+    lax.fori_loop(0, 8, unpack_last, 0)
+    for a, ref in ((0, o_q), (3, o_k), (1, o_v), (2, o_d)):
+        for h in range(4):
+            wide[pl.ds(h, 1024, stride=4), :] = x[
+                h // 2, pl.ds(h % 2 * 1024, 1024), a * 128 : a * 128 + 128
+            ].astype(F32)
+        ref[...] = wide[...].astype(BF16)
+
+
+def quick(queries, key_rows, value_rows, out_grad, bucket_id):
+    rows = [a.reshape(4096, 128) for a in (queries, key_rows, value_rows, out_grad)]
+    vmem = pl.BlockSpec(memory_space=pltpu.VMEM)
+    n = len(OFFSETS)
+    dma = pltpu.SemaphoreType.DMA
+    outs = pl.pallas_call(
+        kernel,
+        out_shape=[jax.ShapeDtypeStruct((4096, 128), BF16)] * 4
+        + [jax.ShapeDtypeStruct((8, 128), F32)],
+        in_specs=[vmem] * 5,
+        out_specs=[vmem] * 5,
+        scratch_shapes=[
+            pltpu.VMEM((4096, 128), F32),
+            pltpu.VMEM((2, 2048, 512), BF16),
+            pltpu.VMEM((2, SPAN, 512), BF16),
+            pltpu.VMEM((2, 64, 512), BF16),
+            pltpu.VMEM((2, SPAN, 512), BF16),
+            pltpu.VMEM((HOT_ROWS, 512), BF16),
+            pltpu.VMEM((2, SPAN, 512), BF16),
+            pltpu.VMEM((2, 64, 512), BF16),
+            pltpu.VMEM((512, 128), BF16),
+            pltpu.VMEM((512, 128), BF16),
+            pltpu.VMEM((4, 16, 128), BF16),
+            pltpu.VMEM((8, 1024), I32),
+            pltpu.VMEM((1024, 128), I32),
+            pltpu.VMEM((SPAN, 128), BF16),
+            pltpu.VMEM((SPAN, 128), BF16),
+            pltpu.VMEM((128, SPAN), BF16),
+            pltpu.VMEM((128, SPAN), BF16),
+            pltpu.VMEM((SPAN, 128), F32),
+            pltpu.VMEM((SPAN, 128), F32),
+            pltpu.VMEM((SPAN, TQ), F32),
+            pltpu.VMEM((SPAN, TQ), F32),
+            pltpu.VMEM((128, TQ), F32),
+            pltpu.VMEM((128, TQ), F32),
+            dma((4, n)), dma((4, n)), dma((n,)), dma((n,)), dma((4,)), dma((PEERS,)),
+            dma((PEERS,)), dma((4,)), dma((4,)), dma((4,)), dma((4,)),
+        ],
+        compiler_params=pltpu.CompilerParams(
+            collective_id=0, has_side_effects=True, vmem_limit_bytes=60 * 2**20
+        ),
+        name="bucket_layer",
+    )(*rows, bucket_id.T)
+    return [a.reshape(1024, 4, 128) for a in outs[:4]], outs[4][0, 0] > 0
 
 
 def bucket_weights(q_part, k_part, valid, scale):
     span = q_part.shape[0]
-    sorted_index = jnp.arange(span, dtype=jnp.int32)
+    sorted_index = jnp.arange(span, dtype=I32)
     allowed = (sorted_index[None, :] <= sorted_index[:, None]) & (
         (valid[None, :] > 0) | (sorted_index[None, :] == sorted_index[:, None])
     )
-    scores = jnp.dot(q_part, k_part.T, preferred_element_type=jnp.float32) * scale
-    scores = jnp.where(allowed, scores, jnp.float32(-1e30))
+    scores = jnp.dot(q_part, k_part.T, preferred_element_type=F32) * scale
+    scores = jnp.where(allowed, scores, F32(-1e30))
     top = jnp.max(scores, axis=1, keepdims=True)
-    expd = jnp.where(allowed, jnp.exp(scores - top), jnp.float32(0.0))
+    expd = jnp.where(allowed, jnp.exp(scores - top), F32(0.0))
     return expd / jnp.sum(expd, axis=1, keepdims=True)
 
 
 def bucket_forward(block, valid, width):
     scale = 1.0 / math.sqrt(width)
     weights = bucket_weights(block[:, :width], block[:, width : 2 * width], valid, scale)
-    rounded = weights.astype(jnp.bfloat16)
-    return jnp.dot(rounded, block[:, 2 * width :], preferred_element_type=jnp.float32).astype(
-        jnp.bfloat16
+    rounded = weights.astype(BF16)
+    return jnp.dot(rounded, block[:, 2 * width :], preferred_element_type=F32).astype(
+        BF16
     )
 
 
@@ -37,17 +597,17 @@
     k_part = block[:, width : 2 * width]
     v_part = block[:, 2 * width : 3 * width]
     weights = bucket_weights(q_part, k_part, valid, scale)
-    rounded = weights.astype(jnp.bfloat16)
-    dprob = jnp.dot(d_part, v_part.T, preferred_element_type=jnp.float32)
+    rounded = weights.astype(BF16)
+    dprob = jnp.dot(d_part, v_part.T, preferred_element_type=F32)
     delta = jnp.sum(weights * dprob, axis=1, keepdims=True)
-    dscore = (weights * (dprob - delta)).astype(jnp.bfloat16)
-    grad_q = (jnp.dot(dscore, k_part, preferred_element_type=jnp.float32) * scale).astype(
-        jnp.bfloat16
-    )
-    grad_k = (jnp.dot(dscore.T, q_part, preferred_element_type=jnp.float32) * scale).astype(
-        jnp.bfloat16
-    )
-    grad_v = jnp.dot(rounded.T, d_part, preferred_element_type=jnp.float32).astype(jnp.bfloat16)
+    dscore = (weights * (dprob - delta)).astype(BF16)
+    grad_q = (jnp.dot(dscore, k_part, preferred_element_type=F32) * scale).astype(
+        BF16
+    )
+    grad_k = (jnp.dot(dscore.T, q_part, preferred_element_type=F32) * scale).astype(
+        BF16
+    )
+    grad_v = jnp.dot(rounded.T, d_part, preferred_element_type=F32).astype(BF16)
     return (rounded, v_part, grad_q, grad_k, grad_v)
 
 
@@ -56,7 +616,7 @@
     return jnp.concatenate([grad_q, grad_k, grad_v], axis=1)
 
 
-def shards(queries, key_rows, value_rows, out_grad, bucket_id, bucket_slot):
+def slow(queries, key_rows, value_rows, out_grad, bucket_id, bucket_slot):
     peers = lax.axis_size("seq")
     tok_count, group, width = queries.shape
     per_owner = BUCKETS_PER_HEAD // peers
@@ -64,14 +624,14 @@
     total = group * per_owner * span
     owner = bucket_id // per_owner
     local_bucket = bucket_id % per_owner
-    head_index = jnp.arange(group, dtype=jnp.int32)[None, :]
+    head_index = jnp.arange(group, dtype=I32)[None, :]
     flat = (
         (head_index * per_owner + local_bucket) * span + owner * SLOTS_PER_SOURCE + bucket_slot
     ).reshape(-1)
     marks = (
-        jnp.zeros((total,), jnp.bfloat16)
+        jnp.zeros((total,), BF16)
         .at[flat]
-        .set(jnp.bfloat16(1.0))
+        .set(BF16(1.0))
         .reshape(group, per_owner, span)
     )
 
@@ -119,6 +679,15 @@
         gathered[:, :, :width],
         gathered[:, :, width : 2 * width],
         gathered[:, :, 2 * width :],
+    )
+
+
+def shards(queries, key_rows, value_rows, out_grad, bucket_id, bucket_slot):
+    fast, crowded = quick(queries, key_rows, value_rows, out_grad, bucket_id)
+    return lax.cond(
+        crowded,
+        lambda: slow(queries, key_rows, value_rows, out_grad, bucket_id, bucket_slot),
+        lambda: tuple(fast),
     )
 
 

time: 553 us -> 256 us (0.46)
  the two profiles are of different devices: /device:TPU:32 before, /device:TPU:12 now
where the time goes in v1:
time: 256 us
  Pallas kernels  246 us (96%)
  local copies, waits for them, and re-layouts  8.4 us (3%)
    pallas_call x1, Pallas kernels, quick(): pl.pallas_call(kernel, out_shape=[jax.ShapeDtypeStruct((4096, 128), BF16)...  246 us
    unnamed x12, local copies, waits for them, and re-layouts  7.21 us

profile of v1, /device:TPU:12, one launch (start us, length us, event | category | flops | bytes accessed | tf_op | source)
XLA Modules:
  0.0 255.8 jit_solution(4342453192155618320)
XLA Ops:
  0.6 0.0 copy-start.3
  0.6 0.0 copy-start.6
  0.7 245.8 %bucket_layer.1 = (bf16[4096,128]{1,0:T(8,128)(2,1)}, bf16[4096,128]{1,0:T(8,128)(2,1)}, bf16[4096,128]{1,0:T(8,128)(2,1)}, bf16[4096,128]{1,0:T(8,128)(2,1)}, f32[8,128]{1,0:T(8,128)}) custom-call(bf16[4096,128]{1,0:T(8,128)(2,1)} %bitcast.66, bf16[4096,128]{1,0:T(8,128)(2,1)} %bitcast.67, bf16[4096,128]{1,0:T(8,128)(2,1)} %bitcast.68, ...), custom_call_target="tpu_custom_call" | custom-call | tf_op jit(solution)/shard_map/bucket_layer/pallas_call | solution.py:531
  246.5 1.2 slice.30
  248.3 0.0 copy-done.3
  248.3 0.0 copy-done.6
  248.3 0.3 conditional.1
  248.6 0.0 copy-start.1
  248.6 0.0 copy-start.2
  248.6 2.7 %copy.91 = bf16[1024,4,128]{2,1,0:T(4,128)(2,1)} copy(bf16[1024,4,128]{2,1,0:T(4,128)(2,1)} %get-tuple-element.304) | data formatting | bytes 2097152
  251.3 2.6 copy.92
  253.9 0.0 copy-done.1
  253.9 1.0 copy.93
  254.9 0.0 copy-done.2
  254.9 1.0 copy.94
Async XLA Ops:
  0.6 247.7 %copy-start.3 = (s32[1024,4]{0,1:T(4,128)S(1)}, s32[1024,4]{0,1:T(4,128)}, u32[]{:S(2)}) copy-start(s32[1024,4]{0,1:T(4,128)} %param.16) | copy-start | bytes 49156
  0.6 247.7 %copy-start.6 = (s32[1024,4]{0,1:T(4,128)S(1)}, s32[1024,4]{0,1:T(4,128)}, u32[]{:S(2)}) copy-start(s32[1024,4]{0,1:T(4,128)} %param.17) | copy-start | bytes 49156
  248.6 5.3 %copy-start.1 = (bf16[1024,4,128]{2,1,0:T(4,128)(2,1)S(1)}, bf16[1024,4,128]{2,1,0:T(4,128)(2,1)}, u32[]{:S(2)}) copy-start(bf16[1024,4,128]{2,1,0:T(4,128)(2,1)} %get-tuple-element.306) | copy-start | bytes 3145732
  248.6 6.2 %copy-start.2 = (bf16[1024,4,128]{2,1,0:T(4,128)(2,1)S(1)}, bf16[1024,4,128]{2,1,0:T(4,128)(2,1)}, u32[]{:S(2)}) copy-start(bf16[1024,4,128]{2,1,0:T(4,128)(2,1)} %get-tuple-element.307) | copy-start | bytes 3145732

commit v2 on v1

v2 whole, which is shorter than its diff:
```python
import functools
import math

import jax
import jax.numpy as jnp
from jax import lax
from jax.experimental import pallas as pl
from jax.experimental.pallas import tpu as pltpu
from jax.sharding import PartitionSpec as P

SLOTS_PER_SOURCE = 32
BUCKETS_PER_HEAD = 64
PEERS = 32
ROWS = 96
SPAN = PEERS * ROWS
HOT_ROWS = PEERS * SLOTS_PER_SOURCE
HOT_AT = (0, 10, 20, 30)
TQ, TK = 256, 512
HALF = ROWS // 2
WINDOWS = PEERS * 64
SECOND = ((2, 0), (2, 1), (1, 0), (3, 0), (1, 1), (3, 1), (0, 1))
SWITCH = 6
FAR = 2.0**100
MESH = pl.DeviceIdType.MESH
F32, BF16, I32 = jnp.float32, jnp.bfloat16, jnp.int32


def iota(shape, dim):
    return lax.broadcasted_iota(I32, shape, dim)


def dot(a, b, dims=((1,), (0,))):
    return lax.dot_general(a, b, (dims, ((), ())), preferred_element_type=F32)


def kernel(
    q_ref, k_ref, v_ref, d_ref, bid_ref,
    x, flag_out,
    wide, send, send_hot, recv, recv_hot, ret, ret_hot, mid, rows_buf, meta, meta_in, flags,
    pos_row, pos_col, aug_q, aug_k, kt, vt, dk, dv, p_buf, dp_buf, tops, acc_o, acc_q,
    one_ssem, one_rsem, two_ssem, two_rsem, own_sem, free_sem, meta_ssem, meta_rsem,
    hot_ssem, hot_rsem, back_ssem, back_rsem, flag_ssem, flag_rsem,
):
    me = lax.axis_index("seq")
    col = lax.axis_index("head")
    y, z, c = me // 8, lax.rem(me // 2, 4), lax.rem(me, 2)
    scale = 1.0 / math.sqrt(128)
    to_exp2 = scale * math.log2(math.e)

    def ya(d):
        return lax.rem(y + d, 4)

    def za(d):
        return lax.rem(z + d, 4)

    def dev(yy, zz, cc):
        return yy * 8 + zz * 2 + cc

    barrier = pltpu.get_barrier_semaphore()
    for k in range(1, PEERS):
        pl.semaphore_signal(
            barrier, inc=1, device_id={"seq": lax.rem(me + k, PEERS)}, device_id_type=MESH
        )
    for step in (1, 2, 3):
        pl.semaphore_signal(
            barrier, inc=1, device_id={"head": lax.rem(col + step, 4)}, device_id_type=MESH
        )

    for a, ref in enumerate((q_ref, k_ref, v_ref, d_ref)):
        wide[...] = ref[...].astype(F32)
        for h in range(4):
            x[h, :, a * 128 : a * 128 + 128] = wide[
                pl.ds(h, 1024, stride=4), :
            ].astype(BF16)

    named = jnp.concatenate(
        [(iota((64, 1024), 0) == bid_ref[h : h + 1, :]).astype(F32) for h in range(4)], axis=0
    )
    earlier = (iota((1024, 1024), 0) < iota((1024, 1024), 1)).astype(F32).astype(BF16)
    rank = dot(named.astype(BF16), earlier)
    count = jnp.sum(named, axis=1, keepdims=True)
    full = (count == 32.0).astype(F32)
    count = count * (1.0 - full)
    bad = jnp.float32(0.0)
    for h in range(4):
        n_full = jnp.sum(full[h * 64 : h * 64 + 64])
        bad = jnp.maximum(bad, (n_full != 1.0).astype(F32))
    r0, r1 = iota((256, 256), 0), iota((256, 256), 1)
    alike = r0 // 2 == r1 // 2
    lanes = jnp.broadcast_to(count, (256, 128))
    lanes16 = lanes.astype(BF16)
    start = dot((alike & (r1 < r0)).astype(F32).astype(BF16), lanes16)[:, :1]
    both = dot(alike.astype(F32).astype(BF16), lanes16)[:, :1]
    rows = iota((256, 1), 0)
    owner = lax.rem(rows, 64) // 2
    second = lax.rem(rows // 64, 2)
    inside = start + jnp.where(second == 1, ROWS - both, 0.0)
    at_hot = (second * 32).astype(F32)
    base = jnp.where(full > 0, SPAN + at_hot, (owner * ROWS).astype(F32) + inside)
    back = jnp.where(full > 0, WINDOWS + at_hot, (owner * 64 - second * 32).astype(F32) + inside)

    def per_head(table):
        landed = named * (rank + table)
        return jnp.concatenate(
            [jnp.sum(landed[h * 64 : h * 64 + 64], axis=0, keepdims=True) for h in range(4)],
            axis=0,
        )

    pos_row[0:4, :] = per_head(base).astype(I32)
    place = jnp.concatenate([per_head(back), jnp.zeros((124, 1024), F32)], axis=0)
    pos_col[...] = place.T.astype(I32)

    lane, r2 = iota((256, 128), 1), iota((256, 128), 0)
    code = lax.rem(r2 // 64, 2) * 2 + lax.rem(r2, 2)
    front, rear = code < 2, code >= 2
    low = (lane < 2) | (lane == 4)
    high = (lane == 2) | (lane == 3)
    w_start = jnp.where((low & front & (code < lane)) | (lane == 5), lanes, 0.0)
    w_start = w_start - jnp.where(high & rear & (code >= lane), lanes, 0.0)
    w_end = jnp.where((lane < 2) & front & (code <= lane), lanes, 0.0)
    w_end = w_end - jnp.where((high & (code > lane)) | (lane == 4) & rear, lanes, 0.0)
    mr, mc = iota((512, 256), 0), iota((512, 256), 1)
    mine = mr // 16 == lax.rem(mc, 64) // 2
    pick_start = (mine & (lax.rem(mr, 16) == mc // 128 * 2)).astype(F32).astype(BF16)
    pick_end = (mine & (lax.rem(mr, 16) == mc // 128 * 2 + 1)).astype(F32).astype(BF16)
    starts = dot(pick_start, w_start.astype(BF16))
    kind, ml = lax.rem(iota((512, 128), 0), 16), iota((512, 128), 1)
    bad = jnp.maximum(bad, (jnp.max(jnp.where(ml == 5, starts, 0.0)) > ROWS).astype(F32))
    high = (ml == 2) | (ml == 3)
    to_rows = ((kind == 0) | (kind == 2)) & high
    to_rows = to_rows | ((kind == 1) | (kind == 3)) & (high | (ml == 4))
    tail = jnp.where(to_rows, jnp.float32(ROWS), 0.0) + jnp.where(kind == 4, bad, 0.0)
    meta[...] = (starts + dot(pick_end, w_end.astype(BF16)) + tail).astype(BF16)

    pl.semaphore_wait(barrier, PEERS - 1 + 3)

    def meta_copy(k):
        other = lax.rem(me + k, PEERS)
        return pltpu.make_async_remote_copy(
            src_ref=meta.at[pl.ds(pl.multiple_of(other * 16, 16), 16)],
            dst_ref=meta_in.at[pl.ds(pl.multiple_of(me * 16, 16), 16)],
            send_sem=meta_ssem.at[k],
            recv_sem=meta_rsem.at[k],
            device_id={"seq": other},
            device_id_type=MESH,
        )

    for k in range(1, PEERS):
        meta_copy(k).start()
    own_meta = pl.ds(pl.multiple_of(me * 16, 16), 16)
    meta_in[own_meta, :] = meta[own_meta, :]

    def ends(phase):
        return (send, recv) if phase < 2 else (recv, ret)

    def one(phase, half, d):
        g, src = phase % 2, ends(phase)[0]
        if half == 0:
            from_, to, other = src.at[g, ya(d), :, :, 0:HALF], mid.at[g, 0, y], dev(ya(d), z, c)
        else:
            from_, to, other = src.at[g, :, za(d), :, HALF:ROWS], mid.at[g, 1, z], dev(y, za(d), c)
        return pltpu.make_async_remote_copy(
            src_ref=from_,
            dst_ref=to,
            send_sem=one_ssem.at[phase, half, d],
            recv_sem=one_rsem.at[phase, half, d],
            device_id={"seq": other},
            device_id_type=MESH,
        )

    def one_own(phase, half):
        g, src = phase % 2, ends(phase)[0]
        sem = own_sem.at[phase, half, 0]
        if half == 0:
            return pltpu.make_async_copy(src.at[g, y, :, :, 0:HALF], mid.at[g, 0, y], sem)
        return pltpu.make_async_copy(src.at[g, :, z, :, HALF:ROWS], mid.at[g, 1, z], sem)

    def two(phase, half, d, e):
        g, dst = phase % 2, ends(phase)[1]
        cc = lax.rem(c + e, 2)
        if half == 0:
            from_, to = mid.at[g, 0, :, za(d), cc], dst.at[g, :, z, c, 0:HALF]
            other = dev(y, za(d), cc)
        else:
            from_, to = mid.at[g, 1, :, ya(d), cc], dst.at[g, y, :, c, HALF:ROWS]
            other = dev(ya(d), z, cc)
        return pltpu.make_async_remote_copy(
            src_ref=from_,
            dst_ref=to,
            send_sem=two_ssem.at[phase, half, d * 2 + e],
            recv_sem=two_rsem.at[phase, half, d * 2 + e],
            device_id={"seq": other},
            device_id_type=MESH,
        )

    def two_own(phase, half):
        g, dst = phase % 2, ends(phase)[1]
        sem = own_sem.at[phase, half, 1]
        if half == 0:
            return pltpu.make_async_copy(mid.at[g, 0, :, z, c], dst.at[g, :, z, c, 0:HALF], sem)
        return pltpu.make_async_copy(mid.at[g, 1, :, y, c], dst.at[g, y, :, c, HALF:ROWS], sem)

    def hot_copy(h):
        return pltpu.make_async_remote_copy(
            src_ref=send_hot.at[h // 2, pl.ds(h % 2 * 32, 32)],
            dst_ref=recv_hot.at[pl.ds(pl.multiple_of(me * 32, 32), 32)],
            send_sem=hot_ssem.at[h],
            recv_sem=hot_rsem.at[me],
            device_id={"seq": HOT_AT[h]},
            device_id_type=MESH,
        )

    def hot_from(h, s):
        return pltpu.make_async_remote_copy(
            src_ref=send_hot.at[h // 2, pl.ds(h % 2 * 32, 32)],
            dst_ref=recv_hot.at[pl.ds(s * 32, 32)],
            send_sem=hot_ssem.at[h],
            recv_sem=hot_rsem.at[s],
            device_id={"seq": HOT_AT[h]},
            device_id_type=MESH,
        )

    def hot_own(h):
        return pltpu.make_async_copy(
            send_hot.at[h // 2, pl.ds(h % 2 * 32, 32)],
            recv_hot.at[pl.ds(HOT_AT[h] * 32, 32)],
            hot_ssem.at[h],
        )

    def back_copy(h, s):
        return pltpu.make_async_remote_copy(
            src_ref=recv_hot.at[pl.ds(s * 32, 32)],
            dst_ref=ret_hot.at[h // 2, pl.ds(h % 2 * 32, 32)],
            send_sem=back_ssem.at[s],
            recv_sem=back_rsem.at[h],
            device_id={"seq": s},
            device_id_type=MESH,
        )

    def back_own(h):
        return pltpu.make_async_copy(
            recv_hot.at[pl.ds(HOT_AT[h] * 32, 32)],
            ret_hot.at[h // 2, pl.ds(h % 2 * 32, 32)],
            back_rsem.at[h],
        )

    def start_one(phase):
        if phase >= 2:
            pl.semaphore_wait(free_sem.at[phase % 2], 6)
        for d in (2, 1, 3):
            for half in (0, 1):
                one(phase, half, d).start()
        for half in (0, 1):
            one_own(phase, half).start()
        g = phase % 2
        for h in (2 * g, 2 * g + 1):
            if phase < 2:

                @pl.when(me != HOT_AT[h])
                def _():
                    hot_copy(h).start()

                @pl.when(me == HOT_AT[h])
                def _():
                    hot_own(h).start()

    def start_two(phase):
        for half in (0, 1):
            for d in (1, 2, 3):
                one(phase, half, d).wait_recv()
            one_own(phase, half).wait()
            for d, e in SECOND:
                two(phase, half, d, e).start()
            two_own(phase, half).start()

    def arrive(phase):
        for half in (0, 1):
            for d, e in SECOND:
                two(phase, half, d, e).wait_recv()
            two_own(phase, half).wait()

    def drain(phase):
        for half in (0, 1):
            for d in (1, 2, 3):
                one(phase, half, d).wait_send()
            for d, e in SECOND:
                two(phase, half, d, e).wait_send()
        if phase < 2:
            g = phase % 2
            for d in (1, 2, 3):
                for other in (dev(ya(d), z, c), dev(y, za(d), c)):
                    pl.semaphore_signal(
                        free_sem.at[g], inc=1, device_id={"seq": other}, device_id_type=MESH
                    )
            for h in (2 * g, 2 * g + 1):

                @pl.when(me != HOT_AT[h])
                def _():
                    hot_copy(h).wait_send()

    def back_start(h):
        for s in range(PEERS):
            if s != HOT_AT[h]:
                back_copy(h, s).start()
        back_own(h).start()

    def back_drain(g):
        for h in (2 * g, 2 * g + 1):

            @pl.when(me == HOT_AT[h])
            def _():
                for s in range(PEERS):
                    if s != HOT_AT[h]:
                        back_copy(h, s).wait_send()

    def hot_arrive(h):
        for s in range(PEERS):
            if s != HOT_AT[h]:
                hot_from(h, s).wait_recv()
        hot_own(h).wait()

    def back_arrive(g):
        for h in (2 * g, 2 * g + 1):

            @pl.when(me != HOT_AT[h])
            def _():
                back_copy(h, 0).wait_recv()

            @pl.when(me == HOT_AT[h])
            def _():
                back_own(h).wait()

    def picked(shape, at, first):
        index = iota(shape, 0)
        return (index // 32 * ROWS + lax.rem(index, 32) == at - first).astype(F32).astype(BF16)

    def pack(g):
        a, b = pos_row[2 * g : 2 * g + 1, :], pos_row[2 * g + 1 : 2 * g + 2, :]

        def body(m, _):
            first = m * 16 * ROWS
            two_y = pl.ds(m * 2, 2)
            shape = (2, 4, 2, 32, 512)
            p = picked((512, 1024), a, first)
            send[g, two_y, :, :, 0:32, :] = dot(p, x[2 * g]).astype(BF16).reshape(shape)
            p = picked((512, 1024), b, first + 64)
            send[g, two_y, :, :, 64:96, :] = dot(p, x[2 * g + 1]).astype(BF16).reshape(shape)
            p = picked((512, 1024), a, first + 32)
            t = dot(p, x[2 * g])
            p = picked((512, 1024), b, first + 32)
            t = t + dot(p, x[2 * g + 1])
            send[g, two_y, :, :, 32:64, :] = t.astype(BF16).reshape(shape)
            return 0

        lax.fori_loop(0, 2, body, 0)
        for k, at in ((0, a), (1, b)):
            pick = (iota((32, 1024), 0) + (SPAN + k * 32) == at).astype(F32).astype(BF16)
            send_hot[g, k * 32 : k * 32 + 32] = dot(pick, x[2 * g + k]).astype(BF16)

    def unpack(g):
        def body(m, _):
            t = pl.ds(pl.multiple_of(m * 512, 512), 512)
            for k in (0, 1):
                at = pos_col[t, 2 * g + k : 2 * g + k + 1]
                pick = (iota((512, WINDOWS), 1) == at).astype(F32).astype(BF16)
                hot_pick = (iota((512, 64), 1) + WINDOWS == at).astype(F32).astype(BF16)
                got = ret[g, :, :, :, k * 32 : k * 32 + 64, :].reshape(WINDOWS, 512)
                x[2 * g + k, t, :] = (dot(pick, got) + dot(hot_pick, ret_hot[g])).astype(BF16)
            return 0

        lax.fori_loop(0, 2, body, 0)

    def attend(rows_ref, span, coded, between):
        def body(i, _):
            between(i)
            qs = pl.ds(pl.multiple_of(i * TQ, TQ), TQ)
            q_i = rows_ref[qs, 0:128]
            d_i = rows_ref[qs, 384:512]
            q_a = jnp.concatenate([q_i, aug_q[qs, :]], axis=1) if coded else q_i
            full_tiles = (i * TQ) // TK

            def weigh(j, sums, edge):
                top, total, delta = sums
                ks = pl.ds(pl.multiple_of(j * TK, TK), TK)
                k_j = rows_ref[ks, 128:256]
                if coded:
                    k_j = jnp.concatenate([k_j, aug_k[ks, :]], axis=1)
                s = dot(k_j, q_a, ((1,), (1,)))
                if edge:
                    gap = iota((TK, TQ), 0) - iota((TK, TQ), 1)
                    s = jnp.where(gap <= i * TQ - j * TK, s, -1e30)
                new = jnp.maximum(top, jnp.max(s, axis=0, keepdims=True))
                p = jnp.exp2((s - new) * to_exp2)
                dp = dot(rows_ref[ks, 256:384], d_i, ((1,), (1,)))
                p_buf[ks, :] = p
                dp_buf[ks, :] = dp
                tops[pl.ds(pl.multiple_of(j * 8, 8), 8), :] = jnp.broadcast_to(new, (8, TQ))
                keep = jnp.exp2((top - new) * to_exp2)
                return (
                    new,
                    total * keep + jnp.sum(p, axis=0, keepdims=True),
                    delta * keep + jnp.sum(p * dp, axis=0, keepdims=True),
                )

            none = jnp.zeros((1, TQ), F32)
            sums = (jnp.full((1, TQ), -1e30, F32), none, none)
            sums = lax.fori_loop(0, full_tiles, lambda j, a: weigh(j, a, False), sums)
            top, total, delta = weigh(full_tiles, sums, True)
            inv = 1.0 / total
            delta = delta * inv
            acc_o[...] = jnp.zeros_like(acc_o)
            acc_q[...] = jnp.zeros_like(acc_q)

            def spread(j, _):
                ks = pl.ds(pl.multiple_of(j * TK, TK), TK)
                here = tops[pl.ds(pl.multiple_of(j * 8, 8), 8), :][:1]
                w = p_buf[ks, :] * (jnp.exp2((here - top) * to_exp2) * inv)
                rounded = w.astype(BF16)
                ds = (w * (dp_buf[ks, :] - delta)).astype(BF16)
                acc_o[...] += dot(vt[:, ks], rounded)
                acc_q[...] += dot(kt[:, ks], ds)
                dv[ks, :] += dot(rounded, d_i)
                dk[ks, :] += dot(ds, q_i)
                return 0

            lax.fori_loop(0, full_tiles + 1, spread, 0)
            rows_ref[qs, 0:128] = acc_o[...].T.astype(BF16)
            rows_ref[qs, 384:512] = (acc_q[...] * scale).T.astype(BF16)
            return 0

        def ready(j, _):
            ks = pl.ds(pl.multiple_of(j * TK, TK), TK)
            kt[:, ks] = rows_ref[ks, 128:256].astype(F32).T.astype(BF16)
            vt[:, ks] = rows_ref[ks, 256:384].astype(F32).T.astype(BF16)
            dk[ks, :] = jnp.zeros((TK, 128), F32)
            dv[ks, :] = jnp.zeros((TK, 128), F32)
            return 0

        lax.fori_loop(0, span // TK, ready, 0)
        lax.fori_loop(0, span // TQ, body, 0)

        def finish(j, _):
            ks = pl.ds(pl.multiple_of(j * TK, TK), TK)
            rows_ref[ks, 128:256] = (dk[ks, :] * scale).astype(BF16)
            rows_ref[ks, 256:384] = dv[ks, :].astype(BF16)
            return 0

        lax.fori_loop(0, span // TK, finish, 0)

    def codes(g):
        def body(s, _):
            note = meta_in[pl.ds(pl.multiple_of(s * 16, 16), 16), :].astype(F32)
            r = iota((ROWS, 128), 0).astype(F32)
            inside = (r >= note[2 * g : 2 * g + 1]) & (r < note[2 * g + 1 : 2 * g + 2])
            known = iota((ROWS, 128), 1) <= 4
            at = pl.ds(pl.multiple_of(s * ROWS, ROWS), ROWS)
            aug_q[at, :] = jnp.where(inside, 1.0, 0.0).astype(BF16)
            aug_k[at, :] = jnp.where(known & ~inside, -FAR, 0.0).astype(BF16)
            return 0

        lax.fori_loop(0, PEERS, body, 0)

    def hot_work(g):
        for h in (2 * g, 2 * g + 1):

            @pl.when(me == HOT_AT[h])
            def _():
                hot_arrive(h)
                attend(recv_hot, HOT_ROWS, False, lambda i: None)
                back_start(h)

    def work(g, between):
        def load(yy, _):
            at = pl.ds(pl.multiple_of(yy * 768, 768), 768)
            rows_buf[at, :] = recv[g, yy].reshape(768, 512)
            return 0

        def store(yy, _):
            at = pl.ds(pl.multiple_of(yy * 768, 768), 768)
            recv[g, yy] = rows_buf[at, :].reshape(4, 2, ROWS, 512)
            return 0

        lax.fori_loop(0, 4, load, 0)
        attend(rows_buf, SPAN, True, between)
        lax.fori_loop(0, 4, store, 0)

    def at_block(index, act):
        def between(i):
            @pl.when(i == index)
            def _():
                act()

        return between

    pack(0)
    start_one(0)
    pack(1)
    start_two(0)
    start_one(1)

    for k in range(1, PEERS):
        meta_copy(k).wait()
    noted = meta_in[...].astype(F32)
    noted = jnp.where(lax.rem(iota((512, 128), 0), 16) == 4, noted, 0.0)
    flags[0] = jnp.broadcast_to(jnp.max(noted, axis=0, keepdims=True), (16, 128)).astype(BF16)

    def flag_copy(step):
        return pltpu.make_async_remote_copy(
            src_ref=flags.at[0],
            dst_ref=flags.at[step],
            send_sem=flag_ssem.at[step],
            recv_sem=flag_rsem.at[step],
            device_id={"head": lax.rem(col + step, 4)},
            device_id_type=MESH,
        )

    for step in (1, 2, 3):
        flag_copy(step).start()

    codes(0)
    arrive(0)
    drain(0)
    work(0, at_block(SWITCH, lambda: start_two(1)))
    start_one(2)
    hot_work(0)
    codes(1)
    arrive(1)
    drain(1)
    work(1, at_block(SWITCH, lambda: start_two(2)))
    start_one(3)
    hot_work(1)
    arrive(2)
    start_two(3)
    back_arrive(0)
    unpack(0)
    for step in (1, 2, 3):
        flag_copy(step).wait()
    any_flag = jnp.maximum(
        jnp.maximum(flags[0].astype(F32), flags[1].astype(F32)),
        jnp.maximum(flags[2].astype(F32), flags[3].astype(F32)),
    )
    flag_out[...] = any_flag[:8]
    drain(2)
    back_drain(0)
    arrive(3)
    back_arrive(1)
    unpack(1)
    drain(3)
    back_drain(1)


def settle_kernel(x, o_q, o_k, o_v, o_d, wide):
    for a, ref in ((0, o_q), (3, o_k), (1, o_v), (2, o_d)):
        for h in range(4):
            wide[pl.ds(h, 128, stride=4), :] = x[h, :, a * 128 : a * 128 + 128].astype(F32)
        ref[...] = wide[...].astype(BF16)


def settle(x):
    outs = pl.pallas_call(
        settle_kernel,
        grid=(8,),
        out_shape=[jax.ShapeDtypeStruct((4096, 128), BF16)] * 4,
        in_specs=[pl.BlockSpec((4, 128, 512), lambda i: (0, i, 0))],
        out_specs=[pl.BlockSpec((512, 128), lambda i: (i, 0))] * 4,
        scratch_shapes=[pltpu.VMEM((512, 128), F32)],
        name="settle",
    )(x)
    return tuple(a.reshape(1024, 4, 128) for a in outs)


def quick(queries, key_rows, value_rows, out_grad, bucket_id):
    rows = [a.reshape(4096, 128) for a in (queries, key_rows, value_rows, out_grad)]
    vmem = pl.BlockSpec(memory_space=pltpu.VMEM)
    dma = pltpu.SemaphoreType.DMA
    outs = pl.pallas_call(
        kernel,
        out_shape=[
            jax.ShapeDtypeStruct((4, 1024, 512), BF16),
            jax.ShapeDtypeStruct((8, 128), F32),
        ],
        in_specs=[vmem] * 5,
        out_specs=[vmem] * 2,
        scratch_shapes=[
            pltpu.VMEM((4096, 128), F32),
            pltpu.VMEM((2, 4, 4, 2, ROWS, 512), BF16),
            pltpu.VMEM((2, 64, 512), BF16),
            pltpu.VMEM((2, 4, 4, 2, ROWS, 512), BF16),
            pltpu.VMEM((HOT_ROWS, 512), BF16),
            pltpu.VMEM((2, 4, 4, 2, ROWS, 512), BF16),
            pltpu.VMEM((2, 64, 512), BF16),
            pltpu.VMEM((2, 2, 4, 4, 2, HALF, 512), BF16),
            pltpu.VMEM((SPAN, 512), BF16),
            pltpu.VMEM((512, 128), BF16),
            pltpu.VMEM((512, 128), BF16),
            pltpu.VMEM((4, 16, 128), BF16),
            pltpu.VMEM((8, 1024), I32),
            pltpu.VMEM((1024, 128), I32),
            pltpu.VMEM((SPAN, 128), BF16),
            pltpu.VMEM((SPAN, 128), BF16),
            pltpu.VMEM((128, SPAN), BF16),
            pltpu.VMEM((128, SPAN), BF16),
            pltpu.VMEM((SPAN, 128), F32),
            pltpu.VMEM((SPAN, 128), F32),
            pltpu.VMEM((SPAN, TQ), F32),
            pltpu.VMEM((SPAN, TQ), F32),
            pltpu.VMEM((SPAN // TK * 8, TQ), F32),
            pltpu.VMEM((128, TQ), F32),
            pltpu.VMEM((128, TQ), F32),
            dma((4, 2, 4)), dma((4, 2, 4)), dma((4, 2, 8)), dma((4, 2, 8)), dma((4, 2, 2)),
            pltpu.SemaphoreType.REGULAR((2,)), dma((PEERS,)), dma((PEERS,)),
            dma((4,)), dma((PEERS,)), dma((PEERS,)), dma((4,)), dma((4,)), dma((4,)),
        ],
        compiler_params=pltpu.CompilerParams(
            collective_id=0, has_side_effects=True, vmem_limit_bytes=60 * 2**20
        ),
        name="bucket_layer",
    )(*rows, bucket_id.T)
    return outs[0], outs[1][0, 0] > 0


def bucket_weights(q_part, k_part, valid, scale):
    span = q_part.shape[0]
    sorted_index = jnp.arange(span, dtype=I32)
    allowed = (sorted_index[None, :] <= sorted_index[:, None]) & (
        (valid[None, :] > 0) | (sorted_index[None, :] == sorted_index[:, None])
    )
    scores = jnp.dot(q_part, k_part.T, preferred_element_type=F32) * scale
    scores = jnp.where(allowed, scores, F32(-1e30))
    top = jnp.max(scores, axis=1, keepdims=True)
    expd = jnp.where(allowed, jnp.exp(scores - top), F32(0.0))
    return expd / jnp.sum(expd, axis=1, keepdims=True)


def bucket_forward(block, valid, width):
    scale = 1.0 / math.sqrt(width)
    weights = bucket_weights(block[:, :width], block[:, width : 2 * width], valid, scale)
    rounded = weights.astype(BF16)
    return jnp.dot(rounded, block[:, 2 * width :], preferred_element_type=F32).astype(
        BF16
    )


def bucket_backward(block, d_part, valid, width):
    scale = 1.0 / math.sqrt(width)
    q_part = block[:, :width]
    k_part = block[:, width : 2 * width]
    v_part = block[:, 2 * width : 3 * width]
    weights = bucket_weights(q_part, k_part, valid, scale)
    rounded = weights.astype(BF16)
    dprob = jnp.dot(d_part, v_part.T, preferred_element_type=F32)
    delta = jnp.sum(weights * dprob, axis=1, keepdims=True)
    dscore = (weights * (dprob - delta)).astype(BF16)
    grad_q = (jnp.dot(dscore, k_part, preferred_element_type=F32) * scale).astype(
        BF16
    )
    grad_k = (jnp.dot(dscore.T, q_part, preferred_element_type=F32) * scale).astype(
        BF16
    )
    grad_v = jnp.dot(rounded.T, d_part, preferred_element_type=F32).astype(BF16)
    return (rounded, v_part, grad_q, grad_k, grad_v)


def bucket_grads(block, d_part, valid, width):
    rounded, v_part, grad_q, grad_k, grad_v = bucket_backward(block, d_part, valid, width)
    return jnp.concatenate([grad_q, grad_k, grad_v], axis=1)


def slow(queries, key_rows, value_rows, out_grad, bucket_id, bucket_slot):
    peers = lax.axis_size("seq")
    tok_count, group, width = queries.shape
    per_owner = BUCKETS_PER_HEAD // peers
    span = peers * SLOTS_PER_SOURCE
    total = group * per_owner * span
    owner = bucket_id // per_owner
    local_bucket = bucket_id % per_owner
    head_index = jnp.arange(group, dtype=I32)[None, :]
    flat = (
        (head_index * per_owner + local_bucket) * span + owner * SLOTS_PER_SOURCE + bucket_slot
    ).reshape(-1)
    marks = (
        jnp.zeros((total,), BF16)
        .at[flat]
        .set(BF16(1.0))
        .reshape(group, per_owner, span)
    )

    def spread(rows):
        columns = rows.shape[-1]
        placed = jnp.zeros((total, columns), rows.dtype).at[flat].set(rows.reshape(-1, columns))
        return placed.reshape(group, per_owner, span, columns)

    def collect(buffer):
        columns = buffer.shape[-1]
        return buffer.reshape(total, columns)[flat].reshape(tok_count, group, columns)

    joined = jnp.concatenate([queries, key_rows, value_rows], axis=2)
    blocks, valid = (
        lax.all_to_all(spread(joined), "seq", split_axis=2, concat_axis=2, tiled=True),
        lax.all_to_all(marks, "seq", split_axis=2, concat_axis=2, tiled=True),
    )
    flat_blocks = blocks.reshape(-1, span, 3 * width)
    flat_valid = valid.reshape(-1, span)
    attended = lax.map(
        lambda item: bucket_forward(item[0], item[1], width), (flat_blocks, flat_valid)
    )
    attended = lax.all_to_all(
        attended.reshape(group, per_owner, span, width),
        "seq",
        split_axis=2,
        concat_axis=2,
        tiled=True,
    )
    incoming = lax.all_to_all(spread(out_grad), "seq", split_axis=2, concat_axis=2, tiled=True)
    grads = lax.map(
        lambda item: bucket_grads(item[0], item[1], item[2], width),
        (flat_blocks, incoming.reshape(-1, span, width), flat_valid),
    )
    grads = lax.all_to_all(
        grads.reshape(group, per_owner, span, 3 * width),
        "seq",
        split_axis=2,
        concat_axis=2,
        tiled=True,
    )
    gathered = collect(grads)
    return (
        collect(attended),
        gathered[:, :, :width],
        gathered[:, :, width : 2 * width],
        gathered[:, :, 2 * width :],
    )


def shards(queries, key_rows, value_rows, out_grad, bucket_id, bucket_slot):
    packed, crowded = quick(queries, key_rows, value_rows, out_grad, bucket_id)
    return lax.cond(
        crowded,
        lambda: slow(queries, key_rows, value_rows, out_grad, bucket_id, bucket_slot),
        lambda: settle(packed),
    )


def solution(mesh):
    in_specs = (
        P("seq", "head", None),
        P("seq", "head", None),
        P("seq", "head", None),
        P("seq", "head", None),
        P("seq", "head"),
        P("seq", "head"),
    )
    out_specs = (
        P("seq", "head", None),
        P("seq", "head", None),
        P("seq", "head", None),
        P("seq", "head", None),
    )
    return jax.shard_map(shards, mesh=mesh, in_specs=in_specs, out_specs=out_specs, check_vma=False)
```

time: 256 us -> 211 us (0.82)
  the two profiles are of different devices: /device:TPU:12 before, /device:TPU:32 now
where the time goes in v2:
time: 211 us; the launch traced here: 208 us
  Pallas kernels  206 us (98%)
    pallas_call x1, Pallas kernels, quick(): pl.pallas_call(kernel, out_shape=[jax.ShapeDtypeStruct((4, 1024, 512), BF...  199 us
    pallas_call x1, Pallas kernels, settle(): pl.pallas_call(settle_kernel, grid=(8,), out_shape=[jax.ShapeDtypeStruct(...  6.68 us

profile of v2, /device:TPU:32, one launch (start us, length us, event | category | flops | bytes accessed | tf_op | source)
XLA Modules:
  0.0 208.2 jit_solution(4293537976459026966)
XLA Ops:
  0.6 0.0 copy-start.1
  0.6 0.0 copy-start.4
  0.7 199.0 %bucket_layer.1 = (bf16[4,1024,512]{2,1,0:T(8,128)(2,1)}, f32[8,128]{1,0:T(8,128)}) custom-call(bf16[4096,128]{1,0:T(8,128)(2,1)} %bitcast.66, bf16[4096,128]{1,0:T(8,128)(2,1)} %bitcast.67, bf16[4096,128]{1,0:T(8,128)(2,1)} %bitcast.68, bf16[4096,128]{1,0:T(8,128)(2,1)} %bitcast.71, s32[4,1024]{1,0:T(4,128)} %bitcast.73), custom_call_target="tpu_custom_call" | custom-call | tf_op jit(solution)/shard_map/bucket_layer/pallas_call | solution.py:576
  199.7 1.2 slice.30
  201.5 0.0 copy-done.1
  201.5 0.0 copy-done.4
  201.5 6.7 %conditional.1 = (bf16[1024,4,128]{2,1,0:T(4,128)(2,1)}, bf16[1024,4,128]{2,1,0:T(4,128)(2,1)}, bf16[1024,4,128]{2,1,0:T(4,128)(2,1)}, bf16[1024,4,128]{2,1,0:T(4,128)(2,1)}) conditional(s32[]{:T(128)} %bitcast.24, bf16[4,1024,512]{2,1,0:T(8,128)(2,1)} %get-tuple-element.79, (s32[1024,4]{0,1:T(4,128)S(1)}, s32[1024,4]{0,1:T(4,128)S(1)}, ...), branch_computations={%region_0.0_spmd, %region_1.14_spmd} | conditional | flops 1970390016 | bytes 225125440 | solution.py:737
  201.5 6.7 %settle.1 = (bf16[4096,128]{1,0:T(8,128)(2,1)}, bf16[4096,128]{1,0:T(8,128)(2,1)}, bf16[4096,128]{1,0:T(8,128)(2,1)}, bf16[4096,128]{1,0:T(8,128)(2,1)}) custom-call(bf16[4,1024,512]{2,1,0:T(8,128)(2,1)} %x), custom_call_target="tpu_custom_call" | custom-call | tf_op jit(solution)/shard_map/cond/branch_0_fun/settle/pallas_call | solution.py:560
Async XLA Ops:
  0.6 200.9 %copy-start.1 = (s32[1024,4]{0,1:T(4,128)S(1)}, s32[1024,4]{0,1:T(4,128)}, u32[]{:S(2)}) copy-start(s32[1024,4]{0,1:T(4,128)} %param.16) | copy-start | bytes 49156
  0.6 200.9 %copy-start.4 = (s32[1024,4]{0,1:T(4,128)S(1)}, s32[1024,4]{0,1:T(4,128)}, u32[]{:S(2)}) copy-start(s32[1024,4]{0,1:T(4,128)} %param.17) | copy-start | bytes 49156

commit v3 on v2

--- a/solution.py
+++ b/solution.py
@@ -15,11 +15,11 @@
 SPAN = PEERS * ROWS
 HOT_ROWS = PEERS * SLOTS_PER_SOURCE
 HOT_AT = (0, 10, 20, 30)
-TQ, TK = 256, 512
+TQ, TK = 512, 512
 HALF = ROWS // 2
 WINDOWS = PEERS * 64
 SECOND = ((2, 0), (2, 1), (1, 0), (3, 0), (1, 1), (3, 1), (0, 1))
-SWITCH = 6
+SWITCH = (4, 4)
 FAR = 2.0**100
 MESH = pl.DeviceIdType.MESH
 F32, BF16, I32 = jnp.float32, jnp.bfloat16, jnp.int32
@@ -36,10 +36,10 @@
 def kernel(
     q_ref, k_ref, v_ref, d_ref, bid_ref,
     x, flag_out,
-    wide, send, send_hot, recv, recv_hot, ret, ret_hot, mid, rows_buf, meta, meta_in, flags,
-    pos_row, pos_col, aug_q, aug_k, kt, vt, dk, dv, p_buf, dp_buf, tops, acc_o, acc_q,
+    send, send_hot, recv, recv_hot, ret, ret_hot, mid, rows_buf, meta, meta_in, flags,
+    pos_row, pos_col, aug_q, aug_k, kt, vt, dkv, p_buf, dp_buf, tops, acc_o, acc_q,
     one_ssem, one_rsem, two_ssem, two_rsem, own_sem, free_sem, meta_ssem, meta_rsem,
-    hot_ssem, hot_rsem, back_ssem, back_rsem, flag_ssem, flag_rsem,
+    hot_ssem, hot_rsem, back_ssem, back_rsem, flag_ssem, flag_rsem, in_sem,
 ):
     me = lax.axis_index("seq")
     col = lax.axis_index("head")
@@ -66,18 +66,40 @@
             barrier, inc=1, device_id={"head": lax.rem(col + step, 4)}, device_id_type=MESH
         )
 
-    for a, ref in enumerate((q_ref, k_ref, v_ref, d_ref)):
-        wide[...] = ref[...].astype(F32)
+    inputs = (q_ref, k_ref, v_ref, d_ref)
+    quarters = range(4)
+
+    def load(a, part):
+        return pltpu.make_async_copy(
+            inputs[a].at[pl.ds(part * 1024, 1024)],
+            rows_buf.at[pl.ds(a % 3 * 1024, 1024), pl.ds(part * 128, 128)],
+            in_sem.at[a, part],
+        )
+
+    for a in range(3):
+        for part in quarters:
+            load(a, part).start()
+    for a in range(4):
+        for part in quarters:
+            load(a, part).wait()
+            dkv[part * 1024 : part * 1024 + 1024, :] = rows_buf[
+                a % 3 * 1024 : a % 3 * 1024 + 1024, part * 128 : part * 128 + 128
+            ].astype(F32)
+        if a == 0:
+            for part in quarters:
+                load(3, part).start()
         for h in range(4):
-            x[h, :, a * 128 : a * 128 + 128] = wide[
-                pl.ds(h, 1024, stride=4), :
-            ].astype(BF16)
+            x[h, :, a * 128 : a * 128 + 128] = dkv[pl.ds(h, 1024, stride=4), :].astype(BF16)
 
     named = jnp.concatenate(
         [(iota((64, 1024), 0) == bid_ref[h : h + 1, :]).astype(F32) for h in range(4)], axis=0
     )
-    earlier = (iota((1024, 1024), 0) < iota((1024, 1024), 1)).astype(F32).astype(BF16)
-    rank = dot(named.astype(BF16), earlier)
+    named16 = named.astype(BF16)
+    ranks = []
+    for part in quarters:
+        earlier = iota((1024, 256), 0) < iota((1024, 256), 1) + part * 256
+        ranks.append(dot(named16, earlier.astype(F32).astype(BF16)))
+    rank = jnp.concatenate(ranks, axis=1)
     count = jnp.sum(named, axis=1, keepdims=True)
     full = (count == 32.0).astype(F32)
     count = count * (1.0 - full)
@@ -132,8 +154,6 @@
     tail = jnp.where(to_rows, jnp.float32(ROWS), 0.0) + jnp.where(kind == 4, bad, 0.0)
     meta[...] = (starts + dot(pick_end, w_end.astype(BF16)) + tail).astype(BF16)
 
-    pl.semaphore_wait(barrier, PEERS - 1 + 3)
-
     def meta_copy(k):
         other = lax.rem(me + k, PEERS)
         return pltpu.make_async_remote_copy(
@@ -144,11 +164,6 @@
             device_id={"seq": other},
             device_id_type=MESH,
         )
-
-    for k in range(1, PEERS):
-        meta_copy(k).start()
-    own_meta = pl.ds(pl.multiple_of(me * 16, 16), 16)
-    meta_in[own_meta, :] = meta[own_meta, :]
 
     def ends(phase):
         return (send, recv) if phase < 2 else (recv, ret)
@@ -252,17 +267,17 @@
                 one(phase, half, d).start()
         for half in (0, 1):
             one_own(phase, half).start()
-        g = phase % 2
+
+    def hot_start(g):
         for h in (2 * g, 2 * g + 1):
-            if phase < 2:
-
-                @pl.when(me != HOT_AT[h])
-                def _():
-                    hot_copy(h).start()
-
-                @pl.when(me == HOT_AT[h])
-                def _():
-                    hot_own(h).start()
+
+            @pl.when(me != HOT_AT[h])
+            def _():
+                hot_copy(h).start()
+
+            @pl.when(me == HOT_AT[h])
+            def _():
+                hot_own(h).start()
 
     def start_two(phase):
         for half in (0, 1):
@@ -371,6 +386,9 @@
         lax.fori_loop(0, 2, body, 0)
 
     def attend(rows_ref, span, coded, between):
+        def after(j):
+            return pl.ds(pl.multiple_of(SPAN + j * TK, TK), TK)
+
         def body(i, _):
             between(i)
             qs = pl.ds(pl.multiple_of(i * TQ, TQ), TQ)
@@ -419,8 +437,8 @@
                 ds = (w * (dp_buf[ks, :] - delta)).astype(BF16)
                 acc_o[...] += dot(vt[:, ks], rounded)
                 acc_q[...] += dot(kt[:, ks], ds)
-                dv[ks, :] += dot(rounded, d_i)
-                dk[ks, :] += dot(ds, q_i)
+                dkv[ks, :] += dot(ds, q_i)
+                dkv[after(j), :] += dot(rounded, d_i)
                 return 0
 
             lax.fori_loop(0, full_tiles + 1, spread, 0)
@@ -432,8 +450,8 @@
             ks = pl.ds(pl.multiple_of(j * TK, TK), TK)
             kt[:, ks] = rows_ref[ks, 128:256].astype(F32).T.astype(BF16)
             vt[:, ks] = rows_ref[ks, 256:384].astype(F32).T.astype(BF16)
-            dk[ks, :] = jnp.zeros((TK, 128), F32)
-            dv[ks, :] = jnp.zeros((TK, 128), F32)
+            dkv[ks, :] = jnp.zeros((TK, 128), F32)
+            dkv[after(j), :] = jnp.zeros((TK, 128), F32)
             return 0
 
         lax.fori_loop(0, span // TK, ready, 0)
@@ -441,8 +459,8 @@
 
         def finish(j, _):
             ks = pl.ds(pl.multiple_of(j * TK, TK), TK)
-            rows_ref[ks, 128:256] = (dk[ks, :] * scale).astype(BF16)
-            rows_ref[ks, 256:384] = dv[ks, :].astype(BF16)
+            rows_ref[ks, 128:256] = (dkv[ks, :] * scale).astype(BF16)
+            rows_ref[ks, 256:384] = dkv[after(j), :].astype(BF16)
             return 0
 
         lax.fori_loop(0, span // TK, finish, 0)
@@ -460,13 +478,21 @@
 
         lax.fori_loop(0, PEERS, body, 0)
 
-    def hot_work(g):
-        for h in (2 * g, 2 * g + 1):
+    def hot_work():
+        for h in range(4):
 
             @pl.when(me == HOT_AT[h])
             def _():
                 hot_arrive(h)
-                attend(recv_hot, HOT_ROWS, False, lambda i: None)
+
+        @pl.when((me == HOT_AT[0]) | (me == HOT_AT[1]) | (me == HOT_AT[2]) | (me == HOT_AT[3]))
+        def _():
+            attend(recv_hot, HOT_ROWS, False, lambda i: None)
+
+        for h in range(4):
+
+            @pl.when(me == HOT_AT[h])
+            def _():
                 back_start(h)
 
     def work(g, between):
@@ -493,10 +519,16 @@
         return between
 
     pack(0)
+    pl.semaphore_wait(barrier, PEERS - 1 + 3)
     start_one(0)
+    hot_start(0)
+    for k in range(1, PEERS):
+        meta_copy(k).start()
+    own_meta = pl.ds(pl.multiple_of(me * 16, 16), 16)
+    meta_in[own_meta, :] = meta[own_meta, :]
     pack(1)
+    hot_start(1)
     start_two(0)
-    start_one(1)
 
     for k in range(1, PEERS):
         meta_copy(k).wait()
@@ -518,21 +550,21 @@
         flag_copy(step).start()
 
     codes(0)
+    hot_work()
     arrive(0)
+    start_one(1)
     drain(0)
-    work(0, at_block(SWITCH, lambda: start_two(1)))
+    work(0, at_block(SWITCH[0], lambda: start_two(1)))
     start_one(2)
-    hot_work(0)
     codes(1)
     arrive(1)
     drain(1)
-    work(1, at_block(SWITCH, lambda: start_two(2)))
+    work(1, at_block(SWITCH[1], lambda: start_two(2)))
     start_one(3)
-    hot_work(1)
     arrive(2)
-    start_two(3)
     back_arrive(0)
     unpack(0)
+    start_two(3)
     for step in (1, 2, 3):
         flag_copy(step).wait()
     any_flag = jnp.maximum(
@@ -549,21 +581,46 @@
     back_drain(1)
 
 
-def settle_kernel(x, o_q, o_k, o_v, o_d, wide):
-    for a, ref in ((0, o_q), (3, o_k), (1, o_v), (2, o_d)):
-        for h in range(4):
-            wide[pl.ds(h, 128, stride=4), :] = x[h, :, a * 128 : a * 128 + 128].astype(F32)
-        ref[...] = wide[...].astype(BF16)
+def settle_kernel(x, o_q, o_k, o_v, o_d, held, wide, done, in_sem, out_sem):
+    def load(m):
+        return pltpu.make_async_copy(x.at[:, pl.ds(m * 256, 256)], held.at[m], in_sem.at[m])
+
+    outs = ((0, o_q), (3, o_k), (1, o_v), (2, o_d))
+
+    def save(m, n):
+        at = pl.ds(m * 1024, 1024)
+        return pltpu.make_async_copy(done.at[n, at], outs[n][1].at[at], out_sem.at[m, n])
+
+    for m in range(4):
+        load(m).start()
+    for m in range(4):
+        load(m).wait()
+        for n, (a, _) in enumerate(outs):
+            for h in range(4):
+                wide[n, pl.ds(h, 256, stride=4), :] = held[m, h, :, a * 128 : a * 128 + 128].astype(
+                    F32
+                )
+            done[n, m * 1024 : m * 1024 + 1024, :] = wide[n].astype(BF16)
+            save(m, n).start()
+    for m in range(4):
+        for n in range(4):
+            save(m, n).wait()
 
 
 def settle(x):
     outs = pl.pallas_call(
         settle_kernel,
-        grid=(8,),
         out_shape=[jax.ShapeDtypeStruct((4096, 128), BF16)] * 4,
-        in_specs=[pl.BlockSpec((4, 128, 512), lambda i: (0, i, 0))],
-        out_specs=[pl.BlockSpec((512, 128), lambda i: (i, 0))] * 4,
-        scratch_shapes=[pltpu.VMEM((512, 128), F32)],
+        in_specs=[pl.BlockSpec(memory_space=pl.ANY)],
+        out_specs=[pl.BlockSpec(memory_space=pl.ANY)] * 4,
+        scratch_shapes=[
+            pltpu.VMEM((4, 4, 256, 512), BF16),
+            pltpu.VMEM((4, 1024, 128), F32),
+            pltpu.VMEM((4, 4096, 128), BF16),
+            pltpu.SemaphoreType.DMA((4,)),
+            pltpu.SemaphoreType.DMA((4, 4)),
+        ],
+        compiler_params=pltpu.CompilerParams(vmem_limit_bytes=32 * 2**20),
         name="settle",
     )(x)
     return tuple(a.reshape(1024, 4, 128) for a in outs)
@@ -579,10 +636,9 @@
             jax.ShapeDtypeStruct((4, 1024, 512), BF16),
             jax.ShapeDtypeStruct((8, 128), F32),
         ],
-        in_specs=[vmem] * 5,
+        in_specs=[pl.BlockSpec(memory_space=pl.ANY)] * 4 + [vmem],
         out_specs=[vmem] * 2,
         scratch_shapes=[
-            pltpu.VMEM((4096, 128), F32),
             pltpu.VMEM((2, 4, 4, 2, ROWS, 512), BF16),
             pltpu.VMEM((2, 64, 512), BF16),
             pltpu.VMEM((2, 4, 4, 2, ROWS, 512), BF16),
@@ -600,8 +656,7 @@
             pltpu.VMEM((SPAN, 128), BF16),
             pltpu.VMEM((128, SPAN), BF16),
             pltpu.VMEM((128, SPAN), BF16),
-            pltpu.VMEM((SPAN, 128), F32),
-            pltpu.VMEM((SPAN, 128), F32),
+            pltpu.VMEM((2 * SPAN, 128), F32),
             pltpu.VMEM((SPAN, TQ), F32),
             pltpu.VMEM((SPAN, TQ), F32),
             pltpu.VMEM((SPAN // TK * 8, TQ), F32),
@@ -610,6 +665,7 @@
             dma((4, 2, 4)), dma((4, 2, 4)), dma((4, 2, 8)), dma((4, 2, 8)), dma((4, 2, 2)),
             pltpu.SemaphoreType.REGULAR((2,)), dma((PEERS,)), dma((PEERS,)),
             dma((4,)), dma((PEERS,)), dma((PEERS,)), dma((4,)), dma((4,)), dma((4,)),
+            dma((4, 4)),
         ],
         compiler_params=pltpu.CompilerParams(
             collective_id=0, has_side_effects=True, vmem_limit_bytes=60 * 2**20

time: 211 us -> 191 us (0.905)
  Pallas kernels: 206 us -> 186 us
    pallas_call x1, Pallas kernels: 199 us -> 182 us  [quick(): pl.pallas_call(kernel, out_shape=[jax.ShapeDtypeStruct((4, 1024, 512), BF...]
    pallas_call x1, Pallas kernels: 6.68 us -> 3.63 us  [settle(): pl.pallas_call(settle_kernel, out_shape=[jax.ShapeDtypeStruct((4096, 128)...]
where the time goes in v3:
time: 191 us; the launch traced here: 189 us
  Pallas kernels  186 us (97%)
    pallas_call x1, Pallas kernels, quick(): pl.pallas_call(kernel, out_shape=[jax.ShapeDtypeStruct((4, 1024, 512), BF...  182 us

profile of v3, /device:TPU:32, one launch (start us, length us, event | category | flops | bytes accessed | tf_op | source)
XLA Modules:
  0.0 189.1 jit_solution(607155280371295331)
XLA Ops:
  0.6 0.0 copy-start.1
  0.6 0.0 copy-start.4
  0.7 182.4 %bucket_layer.1 = (bf16[4,1024,512]{2,1,0:T(8,128)(2,1)}, f32[8,128]{1,0:T(8,128)}) custom-call(bf16[4096,128]{1,0:T(8,128)(2,1)} %bitcast.66, bf16[4096,128]{1,0:T(8,128)(2,1)} %bitcast.67, bf16[4096,128]{1,0:T(8,128)(2,1)} %bitcast.68, bf16[4096,128]{1,0:T(8,128)(2,1)} %bitcast.71, s32[4,1024]{1,0:T(4,128)} %bitcast.73), custom_call_target="tpu_custom_call" | custom-call | tf_op jit(solution)/shard_map/bucket_layer/pallas_call | solution.py:633
  183.1 1.2 slice.30
  184.9 0.0 copy-done.1
  184.9 0.0 copy-done.4
  184.9 3.9 %conditional.1 = (bf16[1024,4,128]{2,1,0:T(4,128)(2,1)}, bf16[1024,4,128]{2,1,0:T(4,128)(2,1)}, bf16[1024,4,128]{2,1,0:T(4,128)(2,1)}, bf16[1024,4,128]{2,1,0:T(4,128)(2,1)}) conditional(s32[]{:T(128)} %bitcast.24, bf16[4,1024,512]{2,1,0:T(8,128)(2,1)} %get-tuple-element.79, (s32[1024,4]{0,1:T(4,128)S(1)}, s32[1024,4]{0,1:T(4,128)S(1)}, ...), branch_computations={%region_0.0_spmd, %region_1.14_spmd} | conditional | flops 1970390016 | bytes 225125440 | solution.py:793
  185.0 3.6 %settle.1 = (bf16[4096,128]{1,0:T(8,128)(2,1)}, bf16[4096,128]{1,0:T(8,128)(2,1)}, bf16[4096,128]{1,0:T(8,128)(2,1)}, bf16[4096,128]{1,0:T(8,128)(2,1)}) custom-call(bf16[4,1024,512]{2,1,0:T(8,128)(2,1)} %x), custom_call_target="tpu_custom_call" | custom-call | tf_op jit(solution)/shard_map/cond/branch_0_fun/settle/pallas_call | solution.py:611
Async XLA Ops:
  0.6 184.3 %copy-start.1 = (s32[1024,4]{0,1:T(4,128)S(1)}, s32[1024,4]{0,1:T(4,128)}, u32[]{:S(2)}) copy-start(s32[1024,4]{0,1:T(4,128)} %param.16) | copy-start | bytes 49156
  0.6 184.3 %copy-start.4 = (s32[1024,4]{0,1:T(4,128)S(1)}, s32[1024,4]{0,1:T(4,128)}, u32[]{:S(2)}) copy-start(s32[1024,4]{0,1:T(4,128)} %param.17) | copy-start | bytes 49156

commit v4 on v3

--- a/solution.py
+++ b/solution.py
@@ -18,8 +18,8 @@
 TQ, TK = 512, 512
 HALF = ROWS // 2
 WINDOWS = PEERS * 64
-SECOND = ((2, 0), (2, 1), (1, 0), (3, 0), (1, 1), (3, 1), (0, 1))
-SWITCH = (4, 4)
+SECOND = (((2, 0), (1, 0), (3, 0)), ((2, 1), (1, 1), (3, 1), (0, 1)))
+SWITCH = ((3, 4), (3, 4))
 FAR = 2.0**100
 MESH = pl.DeviceIdType.MESH
 F32, BF16, I32 = jnp.float32, jnp.bfloat16, jnp.int32
@@ -168,17 +168,19 @@
     def ends(phase):
         return (send, recv) if phase < 2 else (recv, ret)
 
-    def one(phase, half, d):
-        g, src = phase % 2, ends(phase)[0]
+    def one(phase, half, d, e):
+        g, src, cc = phase % 2, ends(phase)[0], lax.rem(c + e, 2)
         if half == 0:
-            from_, to, other = src.at[g, ya(d), :, :, 0:HALF], mid.at[g, 0, y], dev(ya(d), z, c)
+            from_, to = src.at[g, ya(d), :, cc, 0:HALF], mid.at[g, 0, y, :, cc]
+            other = dev(ya(d), z, c)
         else:
-            from_, to, other = src.at[g, :, za(d), :, HALF:ROWS], mid.at[g, 1, z], dev(y, za(d), c)
+            from_, to = src.at[g, :, za(d), cc, HALF:ROWS], mid.at[g, 1, z, :, cc]
+            other = dev(y, za(d), c)
         return pltpu.make_async_remote_copy(
             src_ref=from_,
             dst_ref=to,
-            send_sem=one_ssem.at[phase, half, d],
-            recv_sem=one_rsem.at[phase, half, d],
+            send_sem=one_ssem.at[phase, half, d * 2 + e],
+            recv_sem=one_rsem.at[phase, half, d * 2 + e],
             device_id={"seq": other},
             device_id_type=MESH,
         )
@@ -262,9 +264,10 @@
     def start_one(phase):
         if phase >= 2:
             pl.semaphore_wait(free_sem.at[phase % 2], 6)
-        for d in (2, 1, 3):
-            for half in (0, 1):
-                one(phase, half, d).start()
+        for e in (0, 1):
+            for d in (2, 1, 3):
+                for half in (0, 1):
+                    one(phase, half, d, e).start()
         for half in (0, 1):
             one_own(phase, half).start()
 
@@ -279,26 +282,31 @@
             def _():
                 hot_own(h).start()
 
-    def start_two(phase):
+    def start_two(phase, e):
         for half in (0, 1):
             for d in (1, 2, 3):
-                one(phase, half, d).wait_recv()
-            one_own(phase, half).wait()
-            for d, e in SECOND:
+                one(phase, half, d, e).wait_recv()
+            if e == 0:
+                one_own(phase, half).wait()
+        for d, _ in SECOND[e]:
+            for half in (0, 1):
                 two(phase, half, d, e).start()
-            two_own(phase, half).start()
+        if e == 0:
+            for half in (0, 1):
+                two_own(phase, half).start()
 
     def arrive(phase):
         for half in (0, 1):
-            for d, e in SECOND:
+            for d, e in SECOND[0] + SECOND[1]:
                 two(phase, half, d, e).wait_recv()
             two_own(phase, half).wait()
 
     def drain(phase):
         for half in (0, 1):
             for d in (1, 2, 3):
-                one(phase, half, d).wait_send()
-            for d, e in SECOND:
+                for e in (0, 1):
+                    one(phase, half, d, e).wait_send()
+            for d, e in SECOND[0] + SECOND[1]:
                 two(phase, half, d, e).wait_send()
         if phase < 2:
             g = phase % 2
@@ -510,11 +518,13 @@
         attend(rows_buf, SPAN, True, between)
         lax.fori_loop(0, 4, store, 0)
 
-    def at_block(index, act):
+    def ahead(phase, blocks):
         def between(i):
-            @pl.when(i == index)
-            def _():
-                act()
+            for e in (0, 1):
+
+                @pl.when(i == blocks[e])
+                def _():
+                    start_two(phase, e)
 
         return between
 
@@ -528,7 +538,9 @@
     meta_in[own_meta, :] = meta[own_meta, :]
     pack(1)
     hot_start(1)
-    start_two(0)
+    start_two(0, 0)
+    start_two(0, 1)
+    start_one(1)
 
     for k in range(1, PEERS):
         meta_copy(k).wait()
@@ -552,19 +564,19 @@
     codes(0)
     hot_work()
     arrive(0)
-    start_one(1)
     drain(0)
-    work(0, at_block(SWITCH[0], lambda: start_two(1)))
+    work(0, ahead(1, SWITCH[0]))
     start_one(2)
     codes(1)
     arrive(1)
     drain(1)
-    work(1, at_block(SWITCH[1], lambda: start_two(2)))
+    work(1, ahead(2, SWITCH[1]))
     start_one(3)
     arrive(2)
+    start_two(3, 0)
     back_arrive(0)
     unpack(0)
-    start_two(3)
+    start_two(3, 1)
     for step in (1, 2, 3):
         flag_copy(step).wait()
     any_flag = jnp.maximum(
@@ -662,7 +674,7 @@
             pltpu.VMEM((SPAN // TK * 8, TQ), F32),
             pltpu.VMEM((128, TQ), F32),
             pltpu.VMEM((128, TQ), F32),
-            dma((4, 2, 4)), dma((4, 2, 4)), dma((4, 2, 8)), dma((4, 2, 8)), dma((4, 2, 2)),
+            dma((4, 2, 8)), dma((4, 2, 8)), dma((4, 2, 8)), dma((4, 2, 8)), dma((4, 2, 2)),
             pltpu.SemaphoreType.REGULAR((2,)), dma((PEERS,)), dma((PEERS,)),
             dma((4,)), dma((PEERS,)), dma((PEERS,)), dma((4,)), dma((4,)), dma((4,)),
             dma((4, 4)),

time: 191 us -> 180 us (0.942)
  Pallas kernels: 186 us -> 176 us
    pallas_call x1, Pallas kernels: 182 us -> 172 us  [quick(): pl.pallas_call(kernel, out_shape=[jax.ShapeDtypeStruct((4, 1024, 512), BF...]
where the time goes in v4:
time: 180 us; the launch traced here: 179 us
  Pallas kernels  176 us (98%)
    pallas_call x1, Pallas kernels, quick(): pl.pallas_call(kernel, out_shape=[jax.ShapeDtypeStruct((4, 1024, 512), BF...  172 us
    pallas_call x1, Pallas kernels, settle(): pl.pallas_call(settle_kernel, out_shape=[jax.ShapeDtypeStruct((4096, 128)...  3.63 us

profile of v4, /device:TPU:32, one launch (start us, length us, event | category | flops | bytes accessed | tf_op | source)
XLA Modules:
  0.0 178.8 jit_solution(14151944887385160731)
XLA Ops:
  0.6 0.0 copy-start.1
  0.6 0.0 copy-start.4
  0.7 172.2 %bucket_layer.1 = (bf16[4,1024,512]{2,1,0:T(8,128)(2,1)}, f32[8,128]{1,0:T(8,128)}) custom-call(bf16[4096,128]{1,0:T(8,128)(2,1)} %bitcast.66, bf16[4096,128]{1,0:T(8,128)(2,1)} %bitcast.67, bf16[4096,128]{1,0:T(8,128)(2,1)} %bitcast.68, bf16[4096,128]{1,0:T(8,128)(2,1)} %bitcast.71, s32[4,1024]{1,0:T(4,128)} %bitcast.73), custom_call_target="tpu_custom_call" | custom-call | tf_op jit(solution)/shard_map/bucket_layer/pallas_call | solution.py:645
  172.9 1.2 slice.30
  174.7 0.0 copy-done.1
  174.7 0.0 copy-done.4
  174.7 3.9 %conditional.1 = (bf16[1024,4,128]{2,1,0:T(4,128)(2,1)}, bf16[1024,4,128]{2,1,0:T(4,128)(2,1)}, bf16[1024,4,128]{2,1,0:T(4,128)(2,1)}, bf16[1024,4,128]{2,1,0:T(4,128)(2,1)}) conditional(s32[]{:T(128)} %bitcast.24, bf16[4,1024,512]{2,1,0:T(8,128)(2,1)} %get-tuple-element.79, (s32[1024,4]{0,1:T(4,128)S(1)}, s32[1024,4]{0,1:T(4,128)S(1)}, ...), branch_computations={%region_0.0_spmd, %region_1.14_spmd} | conditional | flops 1970390016 | bytes 225125440 | solution.py:805
  174.8 3.6 %settle.1 = (bf16[4096,128]{1,0:T(8,128)(2,1)}, bf16[4096,128]{1,0:T(8,128)(2,1)}, bf16[4096,128]{1,0:T(8,128)(2,1)}, bf16[4096,128]{1,0:T(8,128)(2,1)}) custom-call(bf16[4,1024,512]{2,1,0:T(8,128)(2,1)} %x), custom_call_target="tpu_custom_call" | custom-call | tf_op jit(solution)/shard_map/cond/branch_0_fun/settle/pallas_call | solution.py:623
Async XLA Ops:
  0.6 174.1 %copy-start.1 = (s32[1024,4]{0,1:T(4,128)S(1)}, s32[1024,4]{0,1:T(4,128)}, u32[]{:S(2)}) copy-start(s32[1024,4]{0,1:T(4,128)} %param.16) | copy-start | bytes 49156
  0.6 174.1 %copy-start.4 = (s32[1024,4]{0,1:T(4,128)S(1)}, s32[1024,4]{0,1:T(4,128)}, u32[]{:S(2)}) copy-start(s32[1024,4]{0,1:T(4,128)} %param.17) | copy-start | bytes 49156

commit v5 on v4

--- a/solution.py
+++ b/solution.py
@@ -119,7 +119,7 @@
     inside = start + jnp.where(second == 1, ROWS - both, 0.0)
     at_hot = (second * 32).astype(F32)
     base = jnp.where(full > 0, SPAN + at_hot, (owner * ROWS).astype(F32) + inside)
-    back = jnp.where(full > 0, WINDOWS + at_hot, (owner * 64 - second * 32).astype(F32) + inside)
+    back = jnp.where(full > 0, WINDOWS + at_hot, (lax.rem(owner, 2) * 1024 + owner // 2 * 64 - second * 32).astype(F32) + inside)
 
     def per_head(table):
         landed = named * (rank + table)
@@ -261,15 +261,15 @@
             back_rsem.at[h],
         )
 
-    def start_one(phase):
-        if phase >= 2:
+    def start_one(phase, e):
+        if phase >= 2 and e == 0:
             pl.semaphore_wait(free_sem.at[phase % 2], 6)
-        for e in (0, 1):
-            for d in (2, 1, 3):
-                for half in (0, 1):
-                    one(phase, half, d, e).start()
-        for half in (0, 1):
-            one_own(phase, half).start()
+        for d in (2, 1, 3):
+            for half in (0, 1):
+                one(phase, half, d, e).start()
+        if e == 1:
+            for half in (0, 1):
+                one_own(phase, half).start()
 
     def hot_start(g):
         for h in (2 * g, 2 * g + 1):
@@ -295,11 +295,12 @@
             for half in (0, 1):
                 two_own(phase, half).start()
 
-    def arrive(phase):
+    def arrive(phase, e):
         for half in (0, 1):
-            for d, e in SECOND[0] + SECOND[1]:
+            for d, _ in SECOND[e]:
                 two(phase, half, d, e).wait_recv()
-            two_own(phase, half).wait()
+            if e == 0:
+                two_own(phase, half).wait()
 
     def drain(phase):
         for half in (0, 1):
@@ -355,40 +356,43 @@
 
     def picked(shape, at, first):
         index = iota(shape, 0)
-        return (index // 32 * ROWS + lax.rem(index, 32) == at - first).astype(F32).astype(BF16)
-
-    def pack(g):
+        return (index // 32 * (2 * ROWS) + lax.rem(index, 32) == at - first).astype(F32).astype(BF16)
+
+    def pack(g, core):
         a, b = pos_row[2 * g : 2 * g + 1, :], pos_row[2 * g + 1 : 2 * g + 2, :]
 
-        def body(m, _):
-            first = m * 16 * ROWS
-            two_y = pl.ds(m * 2, 2)
-            shape = (2, 4, 2, 32, 512)
-            p = picked((512, 1024), a, first)
-            send[g, two_y, :, :, 0:32, :] = dot(p, x[2 * g]).astype(BF16).reshape(shape)
-            p = picked((512, 1024), b, first + 64)
-            send[g, two_y, :, :, 64:96, :] = dot(p, x[2 * g + 1]).astype(BF16).reshape(shape)
-            p = picked((512, 1024), a, first + 32)
-            t = dot(p, x[2 * g])
-            p = picked((512, 1024), b, first + 32)
-            t = t + dot(p, x[2 * g + 1])
-            send[g, two_y, :, :, 32:64, :] = t.astype(BF16).reshape(shape)
-            return 0
-
-        lax.fori_loop(0, 2, body, 0)
+        shape = (4, 4, 32, 512)
+        first = core * ROWS
+        p = picked((512, 1024), a, first)
+        send[g, :, :, core, 0:32, :] = dot(p, x[2 * g]).astype(BF16).reshape(shape)
+        p = picked((512, 1024), b, first + 64)
+        send[g, :, :, core, 64:96, :] = dot(p, x[2 * g + 1]).astype(BF16).reshape(shape)
+        p = picked((512, 1024), a, first + 32)
+        t = dot(p, x[2 * g])
+        p = picked((512, 1024), b, first + 32)
+        t = t + dot(p, x[2 * g + 1])
+        send[g, :, :, core, 32:64, :] = t.astype(BF16).reshape(shape)
+
+    def pack_hot(g):
+        a, b = pos_row[2 * g : 2 * g + 1, :], pos_row[2 * g + 1 : 2 * g + 2, :]
         for k, at in ((0, a), (1, b)):
             pick = (iota((32, 1024), 0) + (SPAN + k * 32) == at).astype(F32).astype(BF16)
             send_hot[g, k * 32 : k * 32 + 32] = dot(pick, x[2 * g + k]).astype(BF16)
 
-    def unpack(g):
+    def unpack(g, core, last):
         def body(m, _):
             t = pl.ds(pl.multiple_of(m * 512, 512), 512)
             for k in (0, 1):
                 at = pos_col[t, 2 * g + k : 2 * g + k + 1]
-                pick = (iota((512, WINDOWS), 1) == at).astype(F32).astype(BF16)
-                hot_pick = (iota((512, 64), 1) + WINDOWS == at).astype(F32).astype(BF16)
-                got = ret[g, :, :, :, k * 32 : k * 32 + 64, :].reshape(WINDOWS, 512)
-                x[2 * g + k, t, :] = (dot(pick, got) + dot(hot_pick, ret_hot[g])).astype(BF16)
+                pick = (iota((512, 1024), 1) == at - core * 1024).astype(F32).astype(BF16)
+                got = ret[g, :, :, core, k * 32 : k * 32 + 64, :].reshape(1024, 512)
+                got = dot(pick, got)
+                kept = pl.ds(pl.multiple_of(k * 1024 + m * 512, 512), 512)
+                if last:
+                    x[2 * g + k, t, :] = (p_buf[kept, :] + got).astype(BF16)
+                else:
+                    hot_pick = (iota((512, 64), 1) + WINDOWS == at).astype(F32).astype(BF16)
+                    p_buf[kept, :] = got + dot(hot_pick, ret_hot[g])
             return 0
 
         lax.fori_loop(0, 2, body, 0)
@@ -528,19 +532,25 @@
 
         return between
 
-    pack(0)
+    pack(0, c)
     pl.semaphore_wait(barrier, PEERS - 1 + 3)
-    start_one(0)
+    start_one(0, 0)
+    pack(0, 1 - c)
+    start_one(0, 1)
+    pack_hot(0)
     hot_start(0)
     for k in range(1, PEERS):
         meta_copy(k).start()
     own_meta = pl.ds(pl.multiple_of(me * 16, 16), 16)
     meta_in[own_meta, :] = meta[own_meta, :]
-    pack(1)
+    start_two(0, 0)
+    pack(1, c)
+    start_two(0, 1)
+    start_one(1, 0)
+    pack(1, 1 - c)
+    start_one(1, 1)
+    pack_hot(1)
     hot_start(1)
-    start_two(0, 0)
-    start_two(0, 1)
-    start_one(1)
 
     for k in range(1, PEERS):
         meta_copy(k).wait()
@@ -563,20 +573,26 @@
 
     codes(0)
     hot_work()
-    arrive(0)
+    arrive(0, 0)
+    arrive(0, 1)
     drain(0)
     work(0, ahead(1, SWITCH[0]))
-    start_one(2)
+    start_one(2, 0)
+    start_one(2, 1)
     codes(1)
-    arrive(1)
+    arrive(1, 0)
+    arrive(1, 1)
     drain(1)
     work(1, ahead(2, SWITCH[1]))
-    start_one(3)
-    arrive(2)
+    start_one(3, 0)
+    start_one(3, 1)
+    arrive(2, 0)
+    arrive(2, 1)
     start_two(3, 0)
     back_arrive(0)
-    unpack(0)
+    unpack(0, c, False)
     start_two(3, 1)
+    unpack(0, 1 - c, True)
     for step in (1, 2, 3):
         flag_copy(step).wait()
     any_flag = jnp.maximum(
@@ -586,9 +602,11 @@
     flag_out[...] = any_flag[:8]
     drain(2)
     back_drain(0)
-    arrive(3)
     back_arrive(1)
-    unpack(1)
+    arrive(3, 0)
+    unpack(1, c, False)
+    arrive(3, 1)
+    unpack(1, 1 - c, True)
     drain(3)
     back_drain(1)
 

time: 180 us -> 183 us (1.017); the launches traced: 179 us -> 180 us
  no operation moved by 1% of the time
where the time goes in v5:
time: 183 us; the launch traced here: 180 us
  Pallas kernels  177 us (97%)
    pallas_call x1, Pallas kernels, quick(): pl.pallas_call(kernel, out_shape=[jax.ShapeDtypeStruct((4, 1024, 512), BF...  173 us

profile of v5, /device:TPU:32, one launch (start us, length us, event | category | flops | bytes accessed | tf_op | source)
XLA Modules:
  0.0 179.8 jit_solution(9347618175480540696)
XLA Ops:
  0.6 0.0 copy-start.1
  0.6 0.0 copy-start.4
  0.7 173.1 %bucket_layer.1 = (bf16[4,1024,512]{2,1,0:T(8,128)(2,1)}, f32[8,128]{1,0:T(8,128)}) custom-call(bf16[4096,128]{1,0:T(8,128)(2,1)} %bitcast.66, bf16[4096,128]{1,0:T(8,128)(2,1)} %bitcast.67, bf16[4096,128]{1,0:T(8,128)(2,1)} %bitcast.68, bf16[4096,128]{1,0:T(8,128)(2,1)} %bitcast.71, s32[4,1024]{1,0:T(4,128)} %bitcast.73), custom_call_target="tpu_custom_call" | custom-call | tf_op jit(solution)/shard_map/bucket_layer/pallas_call | solution.py:663
  173.8 1.2 slice.30
  175.6 0.0 copy-done.1
  175.6 0.0 copy-done.4
  175.6 3.9 %conditional.1 = (bf16[1024,4,128]{2,1,0:T(4,128)(2,1)}, bf16[1024,4,128]{2,1,0:T(4,128)(2,1)}, bf16[1024,4,128]{2,1,0:T(4,128)(2,1)}, bf16[1024,4,128]{2,1,0:T(4,128)(2,1)}) conditional(s32[]{:T(128)} %bitcast.24, bf16[4,1024,512]{2,1,0:T(8,128)(2,1)} %get-tuple-element.79, (s32[1024,4]{0,1:T(4,128)S(1)}, s32[1024,4]{0,1:T(4,128)S(1)}, ...), branch_computations={%region_0.0_spmd, %region_1.14_spmd} | conditional | flops 1970390016 | bytes 225125440 | solution.py:823
  175.6 3.6 %settle.1 = (bf16[4096,128]{1,0:T(8,128)(2,1)}, bf16[4096,128]{1,0:T(8,128)(2,1)}, bf16[4096,128]{1,0:T(8,128)(2,1)}, bf16[4096,128]{1,0:T(8,128)(2,1)}) custom-call(bf16[4,1024,512]{2,1,0:T(8,128)(2,1)} %x), custom_call_target="tpu_custom_call" | custom-call | tf_op jit(solution)/shard_map/cond/branch_0_fun/settle/pallas_call | solution.py:641
Async XLA Ops:
  0.6 175.0 %copy-start.1 = (s32[1024,4]{0,1:T(4,128)S(1)}, s32[1024,4]{0,1:T(4,128)}, u32[]{:S(2)}) copy-start(s32[1024,4]{0,1:T(4,128)} %param.16) | copy-start | bytes 49156
  0.6 175.0 %copy-start.4 = (s32[1024,4]{0,1:T(4,128)S(1)}, s32[1024,4]{0,1:T(4,128)}, u32[]{:S(2)}) copy-start(s32[1024,4]{0,1:T(4,128)} %param.17) | copy-start | bytes 49156
